TPU v7x, 256 devices: a whole 4x4x8 slice. The times are simulated.
256 devices in a mesh: grp: 8 (over x, core), dev: 32 (over z, y).
Axes of the slice: x: 4, y: 4, z: 8, core: 2. Of those that a mesh axis runs over, the one named last changes fastest.
Arguments:
- embed_source: float32 [131072, 256], P(('grp', 'dev')), may hold values from -1 to 1
- embed_target: float32 [131072, 256], P(('grp', 'dev')), may hold values from -1 to 1
- mass_source: float32 [131072], P(('grp', 'dev')), may hold values from 0.3 to 9
- mass_target: float32 [131072], P(('grp', 'dev')), may hold values from 0.3 to 9
- start_source: float32 [131072, 256], P(('grp', 'dev')), may hold values from 0.5 to 8
- start_target: float32 [131072, 256], P(('grp', 'dev')), may hold values from 0.5 to 8
Outputs:
- factor_source: float32 [131072, 256], P(('grp', 'dev'))
- factor_target: float32 [131072, 256], P(('grp', 'dev'))
- inner_marginal: float32 [256], replicated
All inputs are finite; a program needn't handle non-finite values. Where the computation divides by a largest or mean magnitude, that divisor is 1e-20 or more.
Results may differ from a plain program's by a relative error of at most 0.0003.
Values sent between devices are 32-bit elements; how exact they have to be, the bound alone decides.
No kernel may reach another device: no remote copies, remote signals or barrier semaphores. Data moves between devices by JAX's collectives and lax.ppermute only.
A program may use at most 64 MiB of HBM per device.

v0:
```python
import jax
import jax.numpy as jnp
from jax import lax
from jax.sharding import PartitionSpec as P

OUTER = 2
INNER = 8


HIGH = lax.Precision.HIGHEST


def contract_rows(points, factor):
    return lax.dot_general(
        points, factor, (((0,), (0,)), ((), ())), precision=HIGH, preferred_element_type=jnp.float32
    )


def local_terms(source, target, norm_source, norm_target, left, right):
    big = jnp.stack([contract_rows(source, left), contract_rows(target, right)])
    small = jnp.stack(
        [
            jnp.dot(norm_source, left, precision=HIGH),
            jnp.sum(left, 0),
            jnp.dot(norm_target, right, precision=HIGH),
            jnp.sum(right, 0),
        ]
    )
    return (big, small)


def reduce_factors(big, small):
    summed = lax.psum((big, small), ("grp", "dev"))
    return (summed[0], summed[1])


def local(embed_source, embed_target, mass_source, mass_target, start_source, start_target):
    totals = lax.psum((jnp.sum(mass_source), jnp.sum(mass_target)), ("grp", "dev"))
    source_mass = mass_source / totals[0]
    target_mass = mass_target / totals[1]
    left = start_source * (source_mass / jnp.sum(start_source, 1))[:, None]
    right = start_target * (target_mass / jnp.sum(start_target, 1))[:, None]
    rank = left.shape[1]
    middle = jnp.full((rank,), 1.0 / rank, jnp.float32)
    norm_source = jnp.sum(embed_source * embed_source, 1)
    norm_target = jnp.sum(embed_target * embed_target, 1)
    carried = None
    for outer in range(OUTER):
        big, small = local_terms(embed_source, embed_target, norm_source, norm_target, left, right)
        carried = reduce_factors(big, small)
        big, small = carried
        cross_source = big[0]
        cross_target = big[1]
        cost_right = (
            norm_source[:, None] * small[3][None, :]
            + small[2][None, :]
            - 2.0 * jnp.dot(embed_source, cross_target, precision=HIGH)
        )
        cost_left = (
            norm_target[:, None] * small[1][None, :]
            + small[0][None, :]
            - 2.0 * jnp.dot(embed_target, cross_source, precision=HIGH)
        )
        grad_left = cost_right / middle[None, :]
        grad_right = cost_left / middle[None, :]
        diagonal = lax.psum(jnp.sum(left * cost_right, 0), ("grp", "dev"))
        grad_middle = -diagonal / (middle * middle)
        peaks = lax.pmax(
            (jnp.max(jnp.abs(grad_left)), jnp.max(jnp.abs(grad_right))), ("grp", "dev")
        )
        peak = jnp.maximum(jnp.maximum(peaks[0], peaks[1]), jnp.max(jnp.abs(grad_middle)))
        rate = 30.0 / (peak * peak + 1e-06)
        kernel_left = left * jnp.exp(-rate * grad_left)
        kernel_right = right * jnp.exp(-rate * grad_right)
        kernel_middle = middle * jnp.exp(-rate * grad_middle)
        scale_left = jnp.ones((rank,), jnp.float32)
        scale_right = jnp.ones((rank,), jnp.float32)
        for inner in range(INNER):
            row_left = source_mass / jnp.dot(kernel_left, scale_left, precision=HIGH)
            row_right = target_mass / jnp.dot(kernel_right, scale_right, precision=HIGH)
            margins = lax.psum(
                jnp.stack(
                    [
                        jnp.dot(row_left, kernel_left, precision=HIGH),
                        jnp.dot(row_right, kernel_right, precision=HIGH),
                    ]
                ),
                ("grp", "dev"),
            )
            marg_left = margins[0]
            marg_right = margins[1]
            middle = jnp.cbrt(kernel_middle * scale_left * marg_left * scale_right * marg_right)
            scale_left = middle / marg_left
            scale_right = middle / marg_right
        left = row_left[:, None] * kernel_left * scale_left[None, :]
        right = row_right[:, None] * kernel_right * scale_right[None, :]
    total_points = left.shape[0] * lax.axis_size("grp") * lax.axis_size("dev")
    factor = float(total_points * rank)
    return (left * factor, right * factor, middle * float(rank))


def solution(mesh):
    return jax.shard_map(
        local,
        mesh=mesh,
        in_specs=(
            P(("grp", "dev"), None),
            P(("grp", "dev"), None),
            P(("grp", "dev")),
            P(("grp", "dev")),
            P(("grp", "dev"), None),
            P(("grp", "dev"), None),
        ),
        out_specs=(P(("grp", "dev"), None), P(("grp", "dev"), None), P()),
        check_vma=False,
    )
```

profile of v0, /device:TPU:1, one launch (start us, length us, event | category | flops | bytes accessed | tf_op | source)
XLA Modules:
  0.0 2154.7 jit_solution(16946975879322165472)
XLA Ops:
  7.2 1.3 copy.9
  10.9 81.5 %all-reduce = (f32[]{:T(128)}, f32[]{:T(128)}) all-reduce(f32[]{:T(128)} %reduce_sum.113, f32[]{:T(128)} %reduce_sum.108), channel_id=1, replica_groups=mesh['grp'=8,'dev'=32] {'grp','dev'}, use_global_device_ids=true, to_apply=%region_7.0 | all-reduce | flops 2 | bytes 16 | tf_op jit(solution)/shard_map/psum | solution.py:38
  95.4 0.8 pad_maximum_fusion
  97.9 73.1 %psum.170 = f32[4,256]{1,0:T(4,128)S(1)} all-reduce(f32[4,256]{1,0:T(4,128)S(1)} %pad_maximum_fusion.2), channel_id=1, replica_groups=mesh['grp'=8,'dev'=32] {'grp','dev'}, use_global_device_ids=true, to_apply=%region_10.0 | all-reduce | flops 1024 | bytes 8192 | tf_op jit(solution)/shard_map/psum | solution.py:33
  171.0 171.1 %all-reduce.4.cloned.1.call-done = f32[2,256,256]{1,2,0:T(8,128)} async-done(((f32[2,256,256]{1,2,0:T(8,128)}), f32[2,256,256]{1,2,0:T(8,128)}) %all-reduce.4.cloned.1.call-update) | async-done | bytes 524304 | tf_op jit(solution)/shard_map/psum | solution.py:33
  342.1 2.4 abs_reduce_fusion.2
  344.5 2.2 multiply_reduce_fusion.1
  348.1 77.5 %pmax.32 = f32[]{:T(128)} all-reduce(f32[]{:T(128)S(6)} %max.20), channel_id=1, replica_groups=mesh['grp'=8,'dev'=32] {'grp','dev'}, use_global_device_ids=true, to_apply=%region_13.0 | all-reduce | flops 1 | bytes 8 | tf_op jit(solution)/shard_map/pmax | solution.py:68
  425.5 73.2 %psum.172 = f32[256]{0:T(256)S(1)} all-reduce(f32[256]{0:T(256)S(1)} %get-tuple-element.8), channel_id=1, replica_groups=mesh['grp'=8,'dev'=32] {'grp','dev'}, use_global_device_ids=true, to_apply=%region_17.0 | all-reduce | flops 256 | bytes 2048 | tf_op jit(solution)/shard_map/psum | solution.py:66
  500.6 1.2 exponential_multiply_fusion.3
  505.0 74.5 %psum.173 = f32[2,256]{1,0:T(2,128)S(1)} all-reduce(f32[2,256]{1,0:T(2,128)S(1)} %pad_maximum_fusion.4), channel_id=1, replica_groups=mesh['grp'=8,'dev'=32] {'grp','dev'}, use_global_device_ids=true, to_apply=%region_19.0 | all-reduce | flops 512 | bytes 4096 | tf_op jit(solution)/shard_map/psum | solution.py:81
  579.9 0.7 multiply_divide_fusion.28
  581.5 0.7 multiply_divide_fusion.29
  582.7 73.5 %psum.174 = f32[2,256]{1,0:T(2,128)S(1)} all-reduce(f32[2,256]{1,0:T(2,128)S(1)} %pad_maximum_fusion.5), channel_id=1, replica_groups=mesh['grp'=8,'dev'=32] {'grp','dev'}, use_global_device_ids=true, to_apply=%region_20.0 | all-reduce | flops 512 | bytes 4096 | tf_op jit(solution)/shard_map/psum | solution.py:81
  656.6 0.7 multiply_divide_fusion.26
  658.2 0.7 multiply_divide_fusion.27
  659.4 74.2 %psum.175 = f32[2,256]{1,0:T(2,128)S(1)} all-reduce(f32[2,256]{1,0:T(2,128)S(1)} %pad_maximum_fusion.6), channel_id=1, replica_groups=mesh['grp'=8,'dev'=32] {'grp','dev'}, use_global_device_ids=true, to_apply=%region_21.0 | all-reduce | flops 512 | bytes 4096 | tf_op jit(solution)/shard_map/psum | solution.py:81
  734.0 0.7 multiply_divide_fusion.24
  735.6 0.7 multiply_divide_fusion.25
  736.8 73.4 %psum.176 = f32[2,256]{1,0:T(2,128)S(1)} all-reduce(f32[2,256]{1,0:T(2,128)S(1)} %pad_maximum_fusion.7), channel_id=1, replica_groups=mesh['grp'=8,'dev'=32] {'grp','dev'}, use_global_device_ids=true, to_apply=%region_22.0 | all-reduce | flops 512 | bytes 4096 | tf_op jit(solution)/shard_map/psum | solution.py:81
  810.6 0.7 multiply_divide_fusion.22
  812.2 0.7 multiply_divide_fusion.23
  813.4 74.3 %psum.177 = f32[2,256]{1,0:T(2,128)S(1)} all-reduce(f32[2,256]{1,0:T(2,128)S(1)} %pad_maximum_fusion.8), channel_id=1, replica_groups=mesh['grp'=8,'dev'=32] {'grp','dev'}, use_global_device_ids=true, to_apply=%region_23.0 | all-reduce | flops 512 | bytes 4096 | tf_op jit(solution)/shard_map/psum | solution.py:81
  890.8 73.6 %psum.178 = f32[2,256]{1,0:T(2,128)S(1)} all-reduce(f32[2,256]{1,0:T(2,128)S(1)} %pad_maximum_fusion.9), channel_id=1, replica_groups=mesh['grp'=8,'dev'=32] {'grp','dev'}, use_global_device_ids=true, to_apply=%region_24.0 | all-reduce | flops 512 | bytes 4096 | tf_op jit(solution)/shard_map/psum | solution.py:81
  967.6 74.3 %psum.179 = f32[2,256]{1,0:T(2,128)S(1)} all-reduce(f32[2,256]{1,0:T(2,128)S(1)} %pad_maximum_fusion.10), channel_id=1, replica_groups=mesh['grp'=8,'dev'=32] {'grp','dev'}, use_global_device_ids=true, to_apply=%region_25.0 | all-reduce | flops 512 | bytes 4096 | tf_op jit(solution)/shard_map/psum | solution.py:81
  1045.0 73.4 %psum.180 = f32[2,256]{1,0:T(2,128)S(1)} all-reduce(f32[2,256]{1,0:T(2,128)S(1)} %pad_maximum_fusion.11), channel_id=1, replica_groups=mesh['grp'=8,'dev'=32] {'grp','dev'}, use_global_device_ids=true, to_apply=%region_26.0 | all-reduce | flops 512 | bytes 4096 | tf_op jit(solution)/shard_map/psum | solution.py:81
  1120.0 0.7 convolution_bitcast_fusion
  1121.4 0.8 pad_maximum_fusion.1
  1122.2 74.8 %psum.181 = f32[4,256]{1,0:T(4,128)S(1)} all-reduce(f32[4,256]{1,0:T(4,128)S(1)} %pad_maximum_fusion.3), channel_id=1, replica_groups=mesh['grp'=8,'dev'=32] {'grp','dev'}, use_global_device_ids=true, to_apply=%region_29.0 | all-reduce | flops 1024 | bytes 8192 | tf_op jit(solution)/shard_map/psum | solution.py:33
  1197.1 172.9 %all-reduce.6.cloned.1.call-done = f32[2,256,256]{1,2,0:T(8,128)} async-done(((f32[2,256,256]{1,2,0:T(8,128)}), f32[2,256,256]{1,2,0:T(8,128)}) %all-reduce.6.cloned.1.call-update) | async-done | bytes 524304 | tf_op jit(solution)/shard_map/psum | solution.py:33
  1370.0 2.4 abs_reduce_fusion
  1372.4 1.4 multiply_reduce_fusion
  1375.1 77.4 %pmax.33 = f32[]{:T(128)} all-reduce(f32[]{:T(128)S(6)} %max.22), channel_id=1, replica_groups=mesh['grp'=8,'dev'=32] {'grp','dev'}, use_global_device_ids=true, to_apply=%region_32.0 | all-reduce | flops 1 | bytes 8 | tf_op jit(solution)/shard_map/pmax | solution.py:68
  1452.6 73.6 %psum.183 = f32[256]{0:T(256)S(1)} all-reduce(f32[256]{0:T(256)S(1)} %get-tuple-element.6), channel_id=1, replica_groups=mesh['grp'=8,'dev'=32] {'grp','dev'}, use_global_device_ids=true, to_apply=%region_36.0 | all-reduce | flops 256 | bytes 2048 | tf_op jit(solution)/shard_map/psum | solution.py:66
  1526.2 0.7 abs_reduce_fusion.4
  1531.8 74.3 %psum.184 = f32[2,256]{1,0:T(2,128)S(1)} all-reduce(f32[2,256]{1,0:T(2,128)S(1)} %pad_maximum_fusion.12), channel_id=1, replica_groups=mesh['grp'=8,'dev'=32] {'grp','dev'}, use_global_device_ids=true, to_apply=%region_38.0 | all-reduce | flops 512 | bytes 4096 | tf_op jit(solution)/shard_map/psum | solution.py:81
  1609.3 73.5 %psum.185 = f32[2,256]{1,0:T(2,128)S(1)} all-reduce(f32[2,256]{1,0:T(2,128)S(1)} %pad_maximum_fusion.13), channel_id=1, replica_groups=mesh['grp'=8,'dev'=32] {'grp','dev'}, use_global_device_ids=true, to_apply=%region_39.0 | all-reduce | flops 512 | bytes 4096 | tf_op jit(solution)/shard_map/psum | solution.py:81
  1685.9 74.2 %psum.186 = f32[2,256]{1,0:T(2,128)S(1)} all-reduce(f32[2,256]{1,0:T(2,128)S(1)} %pad_maximum_fusion.14), channel_id=1, replica_groups=mesh['grp'=8,'dev'=32] {'grp','dev'}, use_global_device_ids=true, to_apply=%region_40.0 | all-reduce | flops 512 | bytes 4096 | tf_op jit(solution)/shard_map/psum | solution.py:81
  1762.1 0.7 multiply_divide_fusion.9
  1763.3 73.4 %psum.187 = f32[2,256]{1,0:T(2,128)S(1)} all-reduce(f32[2,256]{1,0:T(2,128)S(1)} %pad_maximum_fusion.15), channel_id=1, replica_groups=mesh['grp'=8,'dev'=32] {'grp','dev'}, use_global_device_ids=true, to_apply=%region_41.0 | all-reduce | flops 512 | bytes 4096 | tf_op jit(solution)/shard_map/psum | solution.py:81
  1838.7 0.7 multiply_divide_fusion.7
  1839.9 74.4 %psum.188 = f32[2,256]{1,0:T(2,128)S(1)} all-reduce(f32[2,256]{1,0:T(2,128)S(1)} %pad_maximum_fusion.16), channel_id=1, replica_groups=mesh['grp'=8,'dev'=32] {'grp','dev'}, use_global_device_ids=true, to_apply=%region_42.0 | all-reduce | flops 512 | bytes 4096 | tf_op jit(solution)/shard_map/psum | solution.py:81
  1917.5 73.4 %psum.189 = f32[2,256]{1,0:T(2,128)S(1)} all-reduce(f32[2,256]{1,0:T(2,128)S(1)} %pad_maximum_fusion.17), channel_id=1, replica_groups=mesh['grp'=8,'dev'=32] {'grp','dev'}, use_global_device_ids=true, to_apply=%region_43.0 | all-reduce | flops 512 | bytes 4096 | tf_op jit(solution)/shard_map/psum | solution.py:81
  1994.1 74.3 %psum.190 = f32[2,256]{1,0:T(2,128)S(1)} all-reduce(f32[2,256]{1,0:T(2,128)S(1)} %pad_maximum_fusion.18), channel_id=1, replica_groups=mesh['grp'=8,'dev'=32] {'grp','dev'}, use_global_device_ids=true, to_apply=%region_44.0 | all-reduce | flops 512 | bytes 4096 | tf_op jit(solution)/shard_map/psum | solution.py:81
  2069.1 1.3 multiply_divide_fusion
  2071.5 73.4 %psum.191 = f32[2,256]{1,0:T(2,128)S(1)} all-reduce(f32[2,256]{1,0:T(2,128)S(1)} %pad_maximum_fusion.19), channel_id=1, replica_groups=mesh['grp'=8,'dev'=32] {'grp','dev'}, use_global_device_ids=true, to_apply=%region_45.0 | all-reduce | flops 512 | bytes 4096 | tf_op jit(solution)/shard_map/psum | solution.py:81
  2145.7 1.0 copy.12
  2146.7 1.0 copy.11
  (186 shorter events, 53.9 us)
Async XLA Ops:
  7.2 1.4 copy-start.2
  7.2 334.9 %all-reduce.4.cloned.1.call-start = ((), (), s32[]{:S(2)}) async-start(), calls=%async_computation | async-start | bytes 1048576 | tf_op jit(solution)/shard_map/psum | solution.py:33
  8.5 0.7 copy-start.5
  8.5 2.0 copy-start.3
  9.2 0.7 copy-start.4
  10.6 83.0 %copy-start.1 = (f32[512,256]{1,0:T(8,128)S(1)}, f32[512,256]{1,0:T(8,128)}, u32[]{:S(2)}) copy-start(f32[512,256]{1,0:T(8,128)} %param.6) | copy-start | bytes 1572868
  93.7 1.0 copy-start
  96.2 1273.8 %all-reduce.6.cloned.1.call-start = ((), (), s32[]{:S(2)}) async-start(), calls=%async_computation.1 | async-start | bytes 1048576 | tf_op jit(solution)/shard_map/psum | solution.py:33
  342.1 2.4 copy-start.6
  1370.0 2.4 copy-start.7
Sparse Core Ops, SparseCore 0:
  96.3 245.7 all-reduce.3
  1122.3 247.6 all-reduce.5
where the time goes:
time: 2170 us; the launch traced here: 2150 us
  blocking collectives  1710 us (79%)
  waiting for transfers between devices  344 us (16%)
  matrix products  41.9 us (2%)
  other arithmetic  31 us (1%)
    psum x16, blocking collectives, local(): lax.psum(jnp.stack([jnp.dot(row_left, kernel_left, precision=HIGH), jnp.d...  1180 us
    psum x2, waiting for transfers between devices, reduce_factors(): summed = lax.psum((big, small), ('grp', 'dev'))  344 us
    pmax x2, blocking collectives, local(): lax.pmax((jnp.max(jnp.abs(grad_left)), jnp.max(jnp.abs(grad_right))), ('g...  155 us
    psum x2, blocking collectives, reduce_factors(): summed = lax.psum((big, small), ('grp', 'dev'))  148 us
    psum x2, blocking collectives, local(): diagonal = lax.psum(jnp.sum(left * cost_right, 0), ('grp', 'dev'))  147 us
    psum x1, blocking collectives, local(): lax.psum((jnp.sum(mass_source), jnp.sum(mass_target)), ('grp', 'dev'))  81.5 us
  transfers between devices with their start and end apart: 2, of which 2 were waited for; matrix products, arithmetic and copies ran while one was open for 0% of the time, Pallas kernels for 0%

commit v1 on v0

v1 whole, which is shorter than its diff:
```python
import jax
import jax.numpy as jnp
from jax import lax
from jax.sharding import PartitionSpec as P

OUTER = 2
INNER = 8
AXES = ("grp", "dev")
HIGH = lax.Precision.HIGHEST


def contract_rows(a, b):
    return lax.dot_general(a, b, (((0,), (0,)), ((), ())), precision=HIGH, preferred_element_type=jnp.float32)


def exchange(value, axes, size):
    return lax.all_to_all(jnp.broadcast_to(value[None], (size,) + value.shape), axes, 0, 0)


def sum_all(value):
    value = jnp.sum(exchange(value, "grp", lax.axis_size("grp")), 0)
    return jnp.sum(exchange(value, "dev", lax.axis_size("dev")), 0)


def sum_columns(first, second, small):
    rank, width = first.shape
    count = lax.axis_size("grp") * lax.axis_size("dev")
    share = rank // count
    pad = jnp.zeros((rank, 128 - small.shape[0]), jnp.float32)
    packed = jnp.concatenate([first, second, small.T, pad], 1)
    total = packed.shape[1]
    part = jnp.sum(lax.all_to_all(packed.reshape(count, share, total), AXES, 0, 0), 0)
    full = exchange(part, AXES, count).reshape(rank, total)
    return full[:, :width], full[:, width : 2 * width], full[:, 2 * width : 2 * width + small.shape[0]].T


def max_all(value):
    count = lax.axis_size("grp") * lax.axis_size("dev")
    return jnp.max(exchange(jnp.broadcast_to(value, (2,)), AXES, count))


def local(embed_source, embed_target, mass_source, mass_target, start_source, start_target):
    rank = start_source.shape[1]
    norm_source = jnp.sum(embed_source * embed_source, 1)
    norm_target = jnp.sum(embed_target * embed_target, 1)
    left = start_source * (mass_source / jnp.sum(start_source, 1))[:, None]
    right = start_target * (mass_target / jnp.sum(start_target, 1))[:, None]
    middle = jnp.full((rank,), 1.0 / rank, jnp.float32)
    weights_left, weights_right = left, right
    for outer in range(OUTER):
        small = jnp.stack(
            [
                jnp.dot(norm_source, weights_left, precision=HIGH),
                jnp.sum(weights_left, 0),
                jnp.dot(norm_target, weights_right, precision=HIGH),
                jnp.sum(weights_right, 0),
                jnp.full((rank,), jnp.sum(mass_source)),
                jnp.full((rank,), jnp.sum(mass_target)),
            ]
        )
        cross_source, cross_target, small = sum_columns(
            contract_rows(weights_left, embed_source), contract_rows(weights_right, embed_target), small
        )
        if outer == 0:
            inverse_left = 1.0 / small[4]
            inverse_right = 1.0 / small[5]
            source_mass = mass_source * inverse_left[0]
            target_mass = mass_target * inverse_right[0]
            left = left * inverse_left[0]
            right = right * inverse_right[0]
        else:
            marg_left = small[1]
            marg_right = small[3]
            middle = jnp.cbrt(kernel_middle * scale_left * marg_left * scale_right * marg_right)
            inverse_left = middle / marg_left
            inverse_right = middle / marg_right
            left = weights_left * inverse_left[None, :]
            right = weights_right * inverse_right[None, :]
        cross_source = cross_source * inverse_left[:, None]
        cross_target = cross_target * inverse_right[:, None]
        heavy_source, plain_source = small[0] * inverse_left, small[1] * inverse_left
        heavy_target, plain_target = small[2] * inverse_right, small[3] * inverse_right
        diagonal = (
            heavy_source * plain_target + plain_source * heavy_target - 2.0 * jnp.sum(cross_source * cross_target, 1)
        )
        grad_middle = -diagonal / (middle * middle)
        over = 1.0 / middle
        grad_left = (
            norm_source[:, None] * (plain_target * over)[None, :]
            + (heavy_target * over)[None, :]
            - 2.0
            * lax.dot_general(
                embed_source, cross_target * over[:, None], (((1,), (1,)), ((), ())), precision=HIGH
            )
        )
        grad_right = (
            norm_target[:, None] * (plain_source * over)[None, :]
            + (heavy_source * over)[None, :]
            - 2.0
            * lax.dot_general(
                embed_target, cross_source * over[:, None], (((1,), (1,)), ((), ())), precision=HIGH
            )
        )
        peak = max_all(jnp.maximum(jnp.max(jnp.abs(grad_left)), jnp.max(jnp.abs(grad_right))))
        peak = jnp.maximum(peak, jnp.max(jnp.abs(grad_middle)))
        rate = 30.0 / (peak * peak + 1e-06)
        kernel_left = left * jnp.exp(-rate * grad_left)
        kernel_right = right * jnp.exp(-rate * grad_right)
        kernel_middle = middle * jnp.exp(-rate * grad_middle)
        scale_left = jnp.ones((rank,), jnp.float32)
        scale_right = jnp.ones((rank,), jnp.float32)
        for inner in range(INNER):
            row_left = source_mass / jnp.dot(kernel_left, scale_left, precision=HIGH)
            row_right = target_mass / jnp.dot(kernel_right, scale_right, precision=HIGH)
            if outer < OUTER - 1 and inner == INNER - 1:
                weights_left = row_left[:, None] * kernel_left
                weights_right = row_right[:, None] * kernel_right
                break
            margins = sum_all(
                jnp.stack(
                    [
                        jnp.dot(row_left, kernel_left, precision=HIGH),
                        jnp.dot(row_right, kernel_right, precision=HIGH),
                    ]
                )
            )
            marg_left = margins[0]
            marg_right = margins[1]
            middle = jnp.cbrt(kernel_middle * scale_left * marg_left * scale_right * marg_right)
            scale_left = middle / marg_left
            scale_right = middle / marg_right
    left = row_left[:, None] * kernel_left * scale_left[None, :]
    right = row_right[:, None] * kernel_right * scale_right[None, :]
    total_points = left.shape[0] * lax.axis_size("grp") * lax.axis_size("dev")
    factor = float(total_points * rank)
    return (left * factor, right * factor, middle * float(rank))


def solution(mesh):
    return jax.shard_map(
        local,
        mesh=mesh,
        in_specs=(
            P(AXES, None),
            P(AXES, None),
            P(AXES),
            P(AXES),
            P(AXES, None),
            P(AXES, None),
        ),
        out_specs=(P(AXES, None), P(AXES, None), P()),
        check_vma=False,
    )
```

time: 2170 us -> 561 us (0.26)
  blocking collectives: 1710 us -> 444 us
  waiting for transfers between devices: 344 us -> 19.7 us
    psum x21 -> x0, blocking collectives: 1560 us -> none  [the longest x16 1180 us: local(): lax.psum(jnp.stack([jnp.dot(row_left, kernel_left, precision=HIGH), jnp.d...]
    all_to_all x0 -> x34, blocking collectives: none -> 444 us  [the longest x32 376 us: exchange(): lax.all_to_all(jnp.broadcast_to(value[None], (size,) + value.shape), axes...]
    psum x2 -> x0, waiting for transfers between devices: 344 us -> none  [reduce_factors(): summed = lax.psum((big, small), ('grp', 'dev'))]
    pmax x2 -> x0, blocking collectives: 155 us -> none  [local(): lax.pmax((jnp.max(jnp.abs(grad_left)), jnp.max(jnp.abs(grad_right))), ('g...]
where the time goes in v1:
time: 561 us; the launch traced here: 552 us
  blocking collectives  444 us (79%)
  matrix products  43.1 us (8%)
  waiting for transfers between devices  19.7 us (4%)
  local copies, waits for them, and re-layouts  14.4 us (3%)
  other arithmetic  12.5 us (2%)
  starting transfers between devices  10.6 us (2%)
  between operations  7.19 us (1%)
    all_to_all x32, blocking collectives, exchange(): lax.all_to_all(jnp.broadcast_to(value[None], (size,) + value.shape), axes...  376 us
    all_to_all x2, blocking collectives, sum_columns(): lax.all_to_all(packed.reshape(count, share, total), AXES, 0, 0)  68.3 us
    all_to_all x2, waiting for transfers between devices, exchange(): lax.all_to_all(jnp.broadcast_to(value[None], (size,) + value.shape), axes...  19.7 us
  transfers between devices with their start and end apart: 2, of which 2 were waited for; matrix products, arithmetic and copies ran while one was open for 0% of the time, Pallas kernels for 0%

profile of v1, /device:TPU:1, one launch (start us, length us, event | category | flops | bytes accessed | tf_op | source)
XLA Modules:
  0.0 551.6 jit_solution(3225394551718427188)
XLA Ops:
  0.6 1.3 copy.36
  6.9 1.0 fusion.22
  10.6 1.1 copy.37
  11.7 38.6 %all_to_all.182 = f32[256,1,640]{2,1,0:T(1,128)S(1)} all-to-all(f32[256,1,640]{2,1,0:T(1,128)} %copy.37), channel_id=1, replica_groups=mesh['grp'=8,'dev'=32] {'grp','dev'}, dimensions={0} | all-to-all | bytes 1310720 | tf_op jit(solution)/shard_map/all_to_all | solution.py:32
  51.2 29.0 %all_to_all.183 = f32[256,1,640]{2,1,0:T(1,128)} all-to-all(f32[256,1,640]{2,1,0:T(1,128)S(1)} %broadcast_in_dim.68), channel_id=1, replica_groups=mesh['grp'=8,'dev'=32] {'grp','dev'}, dimensions={0} | all-to-all | bytes 1310720 | tf_op jit(solution)/shard_map/all_to_all | solution.py:17
  80.2 1.3 copy.38
  81.7 2.5 abs_reduce_fusion.2
  84.2 2.4 abs_reduce_fusion.3
  88.7 6.7 %all-to-all-start.2 = ((f32[256,1,2]{2,1,0:T(1,128)}), f32[256,1,2]{2,1,0:T(1,128)S(1)}, u32[]{:S(2)}, u32[]{:S(2)}) async-start(f32[256,1,2]{2,1,0:T(1,128)} %broadcast_in_dim_broadcast_in_dim_broadcast_in_dim.6), calls=%async_computation.2 | async-start | bytes 262144 | tf_op jit(solution)/shard_map/all_to_all | solution.py:17
  97.1 10.8 %all-to-all-done.2 = f32[256,1,2]{2,1,0:T(1,128)S(1)} async-done(((f32[256,1,2]{2,1,0:T(1,128)}), f32[256,1,2]{2,1,0:T(1,128)S(1)}, u32[]{:S(2)}, u32[]{:S(2)}) %all-to-all-start.2) | async-done | bytes 2080 | tf_op jit(solution)/shard_map/all_to_all | solution.py:17
  114.8 8.1 %all_to_all.184 = f32[8,2,256]{2,1,0:T(2,128)S(1)} all-to-all(f32[8,2,256]{2,1,0:T(2,128)S(1)} %broadcast_in_dim.70), channel_id=1, replica_groups=mesh['grp'=8,'dev'=32] {'grp'}, dimensions={0} | all-to-all | bytes 32768 | tf_op jit(solution)/shard_map/all_to_all | solution.py:17
  123.6 3.9 all-to-all-start.4
  127.5 8.9 %all-to-all-done.4 = f32[32,2,256]{2,1,0:T(2,128)S(1)} async-done(((f32[32,2,256]{2,1,0:T(2,128)}), f32[32,2,256]{2,1,0:T(2,128)S(1)}, u32[]{:S(2)}, u32[]{:S(2)}) %all-to-all-start.4) | async-done | bytes 65568 | tf_op jit(solution)/shard_map/all_to_all | solution.py:17
  138.4 8.9 %all_to_all.185 = f32[8,2,256]{2,1,0:T(2,128)S(1)} all-to-all(f32[8,2,256]{2,1,0:T(2,128)S(1)} %broadcast_in_dim.72), channel_id=1, replica_groups=mesh['grp'=8,'dev'=32] {'grp'}, dimensions={0} | all-to-all | bytes 32768 | tf_op jit(solution)/shard_map/all_to_all | solution.py:17
  147.3 11.8 %all_to_all.186 = f32[32,2,256]{2,1,0:T(2,128)S(1)} all-to-all(f32[32,2,256]{2,1,0:T(2,128)S(1)} %broadcast_in_dim.73), channel_id=1, replica_groups=mesh['grp'=8,'dev'=32] {'dev'}, dimensions={0} | all-to-all | bytes 131072 | tf_op jit(solution)/shard_map/all_to_all | solution.py:17
  161.1 8.9 %all_to_all.187 = f32[8,2,256]{2,1,0:T(2,128)S(1)} all-to-all(f32[8,2,256]{2,1,0:T(2,128)S(1)} %broadcast_in_dim.74), channel_id=1, replica_groups=mesh['grp'=8,'dev'=32] {'grp'}, dimensions={0} | all-to-all | bytes 32768 | tf_op jit(solution)/shard_map/all_to_all | solution.py:17
  170.0 11.9 %all_to_all.188 = f32[32,2,256]{2,1,0:T(2,128)S(1)} all-to-all(f32[32,2,256]{2,1,0:T(2,128)S(1)} %broadcast_in_dim.75), channel_id=1, replica_groups=mesh['grp'=8,'dev'=32] {'dev'}, dimensions={0} | all-to-all | bytes 131072 | tf_op jit(solution)/shard_map/all_to_all | solution.py:17
  183.9 8.9 %all_to_all.189 = f32[8,2,256]{2,1,0:T(2,128)S(1)} all-to-all(f32[8,2,256]{2,1,0:T(2,128)S(1)} %broadcast_in_dim.76), channel_id=1, replica_groups=mesh['grp'=8,'dev'=32] {'grp'}, dimensions={0} | all-to-all | bytes 32768 | tf_op jit(solution)/shard_map/all_to_all | solution.py:17
  192.8 11.9 %all_to_all.190 = f32[32,2,256]{2,1,0:T(2,128)S(1)} all-to-all(f32[32,2,256]{2,1,0:T(2,128)S(1)} %broadcast_in_dim.77), channel_id=1, replica_groups=mesh['grp'=8,'dev'=32] {'dev'}, dimensions={0} | all-to-all | bytes 131072 | tf_op jit(solution)/shard_map/all_to_all | solution.py:17
  206.7 8.9 %all_to_all.191 = f32[8,2,256]{2,1,0:T(2,128)S(1)} all-to-all(f32[8,2,256]{2,1,0:T(2,128)S(1)} %broadcast_in_dim.78), channel_id=1, replica_groups=mesh['grp'=8,'dev'=32] {'grp'}, dimensions={0} | all-to-all | bytes 32768 | tf_op jit(solution)/shard_map/all_to_all | solution.py:17
  215.6 12.1 %all_to_all.192 = f32[32,2,256]{2,1,0:T(2,128)S(1)} all-to-all(f32[32,2,256]{2,1,0:T(2,128)S(1)} %broadcast_in_dim.79), channel_id=1, replica_groups=mesh['grp'=8,'dev'=32] {'dev'}, dimensions={0} | all-to-all | bytes 131072 | tf_op jit(solution)/shard_map/all_to_all | solution.py:17
  229.7 8.9 %all_to_all.193 = f32[8,2,256]{2,1,0:T(2,128)S(1)} all-to-all(f32[8,2,256]{2,1,0:T(2,128)S(1)} %broadcast_in_dim.80), channel_id=1, replica_groups=mesh['grp'=8,'dev'=32] {'grp'}, dimensions={0} | all-to-all | bytes 32768 | tf_op jit(solution)/shard_map/all_to_all | solution.py:17
  238.6 11.9 %all_to_all.194 = f32[32,2,256]{2,1,0:T(2,128)S(1)} all-to-all(f32[32,2,256]{2,1,0:T(2,128)S(1)} %broadcast_in_dim.81), channel_id=1, replica_groups=mesh['grp'=8,'dev'=32] {'dev'}, dimensions={0} | all-to-all | bytes 131072 | tf_op jit(solution)/shard_map/all_to_all | solution.py:17
  252.5 8.9 %all_to_all.195 = f32[8,2,256]{2,1,0:T(2,128)S(1)} all-to-all(f32[8,2,256]{2,1,0:T(2,128)S(1)} %broadcast_in_dim.82), channel_id=1, replica_groups=mesh['grp'=8,'dev'=32] {'grp'}, dimensions={0} | all-to-all | bytes 32768 | tf_op jit(solution)/shard_map/all_to_all | solution.py:17
  261.4 11.9 %all_to_all.196 = f32[32,2,256]{2,1,0:T(2,128)S(1)} all-to-all(f32[32,2,256]{2,1,0:T(2,128)S(1)} %broadcast_in_dim.83), channel_id=1, replica_groups=mesh['grp'=8,'dev'=32] {'dev'}, dimensions={0} | all-to-all | bytes 131072 | tf_op jit(solution)/shard_map/all_to_all | solution.py:17
  273.8 1.0 fusion.10
  275.8 1.0 fusion.14
  278.2 29.7 %all_to_all.197 = f32[256,1,640]{2,1,0:T(1,128)S(1)} all-to-all(f32[256,1,640]{2,1,0:T(1,128)S(1)} %copy.54), channel_id=1, replica_groups=mesh['grp'=8,'dev'=32] {'grp','dev'}, dimensions={0} | all-to-all | bytes 1310720 | tf_op jit(solution)/shard_map/all_to_all | solution.py:32
  308.7 29.1 %all_to_all.198 = f32[256,1,640]{2,1,0:T(1,128)S(1)} all-to-all(f32[256,1,640]{2,1,0:T(1,128)S(1)} %broadcast_in_dim.85), channel_id=1, replica_groups=mesh['grp'=8,'dev'=32] {'grp','dev'}, dimensions={0} | all-to-all | bytes 1310720 | tf_op jit(solution)/shard_map/all_to_all | solution.py:17
  339.3 1.7 abs_reduce_fusion
  341.0 2.4 abs_reduce_fusion.1
  344.9 18.5 %all_to_all.199 = f32[256,1,2]{2,1,0:T(1,128)S(1)} all-to-all(f32[256,1,2]{2,1,0:T(1,128)S(1)} %broadcast_in_dim_broadcast_in_dim_broadcast_in_dim.7), channel_id=1, replica_groups=mesh['grp'=8,'dev'=32] {'grp','dev'}, dimensions={0} | all-to-all | bytes 4096 | tf_op jit(solution)/shard_map/all_to_all | solution.py:17
  367.8 8.1 %all_to_all.200 = f32[8,2,256]{2,1,0:T(2,128)S(1)} all-to-all(f32[8,2,256]{2,1,0:T(2,128)S(1)} %broadcast_in_dim.86), channel_id=1, replica_groups=mesh['grp'=8,'dev'=32] {'grp'}, dimensions={0} | all-to-all | bytes 32768 | tf_op jit(solution)/shard_map/all_to_all | solution.py:17
  375.9 12.0 %all_to_all.201 = f32[32,2,256]{2,1,0:T(2,128)S(1)} all-to-all(f32[32,2,256]{2,1,0:T(2,128)S(1)} %broadcast_in_dim.87), channel_id=1, replica_groups=mesh['grp'=8,'dev'=32] {'dev'}, dimensions={0} | all-to-all | bytes 131072 | tf_op jit(solution)/shard_map/all_to_all | solution.py:17
  389.9 9.1 %all_to_all.202 = f32[8,2,256]{2,1,0:T(2,128)S(1)} all-to-all(f32[8,2,256]{2,1,0:T(2,128)S(1)} %broadcast_in_dim.88), channel_id=1, replica_groups=mesh['grp'=8,'dev'=32] {'grp'}, dimensions={0} | all-to-all | bytes 32768 | tf_op jit(solution)/shard_map/all_to_all | solution.py:17
  399.1 11.9 %all_to_all.203 = f32[32,2,256]{2,1,0:T(2,128)S(1)} all-to-all(f32[32,2,256]{2,1,0:T(2,128)S(1)} %broadcast_in_dim.89), channel_id=1, replica_groups=mesh['grp'=8,'dev'=32] {'dev'}, dimensions={0} | all-to-all | bytes 131072 | tf_op jit(solution)/shard_map/all_to_all | solution.py:17
  413.0 8.9 %all_to_all.204 = f32[8,2,256]{2,1,0:T(2,128)S(1)} all-to-all(f32[8,2,256]{2,1,0:T(2,128)S(1)} %broadcast_in_dim.90), channel_id=1, replica_groups=mesh['grp'=8,'dev'=32] {'grp'}, dimensions={0} | all-to-all | bytes 32768 | tf_op jit(solution)/shard_map/all_to_all | solution.py:17
  421.9 12.2 %all_to_all.205 = f32[32,2,256]{2,1,0:T(2,128)S(1)} all-to-all(f32[32,2,256]{2,1,0:T(2,128)S(1)} %broadcast_in_dim.91), channel_id=1, replica_groups=mesh['grp'=8,'dev'=32] {'dev'}, dimensions={0} | all-to-all | bytes 131072 | tf_op jit(solution)/shard_map/all_to_all | solution.py:17
  436.0 8.9 %all_to_all.206 = f32[8,2,256]{2,1,0:T(2,128)S(1)} all-to-all(f32[8,2,256]{2,1,0:T(2,128)S(1)} %broadcast_in_dim.92), channel_id=1, replica_groups=mesh['grp'=8,'dev'=32] {'grp'}, dimensions={0} | all-to-all | bytes 32768 | tf_op jit(solution)/shard_map/all_to_all | solution.py:17
  444.9 11.9 %all_to_all.207 = f32[32,2,256]{2,1,0:T(2,128)S(1)} all-to-all(f32[32,2,256]{2,1,0:T(2,128)S(1)} %broadcast_in_dim.93), channel_id=1, replica_groups=mesh['grp'=8,'dev'=32] {'dev'}, dimensions={0} | all-to-all | bytes 131072 | tf_op jit(solution)/shard_map/all_to_all | solution.py:17
  458.8 8.9 %all_to_all.208 = f32[8,2,256]{2,1,0:T(2,128)S(1)} all-to-all(f32[8,2,256]{2,1,0:T(2,128)S(1)} %broadcast_in_dim.94), channel_id=1, replica_groups=mesh['grp'=8,'dev'=32] {'grp'}, dimensions={0} | all-to-all | bytes 32768 | tf_op jit(solution)/shard_map/all_to_all | solution.py:17
  467.7 11.9 %all_to_all.209 = f32[32,2,256]{2,1,0:T(2,128)S(1)} all-to-all(f32[32,2,256]{2,1,0:T(2,128)S(1)} %broadcast_in_dim.95), channel_id=1, replica_groups=mesh['grp'=8,'dev'=32] {'dev'}, dimensions={0} | all-to-all | bytes 131072 | tf_op jit(solution)/shard_map/all_to_all | solution.py:17
  481.6 8.9 %all_to_all.210 = f32[8,2,256]{2,1,0:T(2,128)S(1)} all-to-all(f32[8,2,256]{2,1,0:T(2,128)S(1)} %broadcast_in_dim.96), channel_id=1, replica_groups=mesh['grp'=8,'dev'=32] {'grp'}, dimensions={0} | all-to-all | bytes 32768 | tf_op jit(solution)/shard_map/all_to_all | solution.py:17
  490.6 11.9 %all_to_all.211 = f32[32,2,256]{2,1,0:T(2,128)S(1)} all-to-all(f32[32,2,256]{2,1,0:T(2,128)S(1)} %broadcast_in_dim.97), channel_id=1, replica_groups=mesh['grp'=8,'dev'=32] {'dev'}, dimensions={0} | all-to-all | bytes 131072 | tf_op jit(solution)/shard_map/all_to_all | solution.py:17
  504.4 8.9 %all_to_all.212 = f32[8,2,256]{2,1,0:T(2,128)S(1)} all-to-all(f32[8,2,256]{2,1,0:T(2,128)S(1)} %broadcast_in_dim.98), channel_id=1, replica_groups=mesh['grp'=8,'dev'=32] {'grp'}, dimensions={0} | all-to-all | bytes 32768 | tf_op jit(solution)/shard_map/all_to_all | solution.py:17
  513.4 11.9 %all_to_all.213 = f32[32,2,256]{2,1,0:T(2,128)S(1)} all-to-all(f32[32,2,256]{2,1,0:T(2,128)S(1)} %broadcast_in_dim.99), channel_id=1, replica_groups=mesh['grp'=8,'dev'=32] {'dev'}, dimensions={0} | all-to-all | bytes 131072 | tf_op jit(solution)/shard_map/all_to_all | solution.py:17
  527.2 8.9 %all_to_all.214 = f32[8,2,256]{2,1,0:T(2,128)S(1)} all-to-all(f32[8,2,256]{2,1,0:T(2,128)S(1)} %broadcast_in_dim.100), channel_id=1, replica_groups=mesh['grp'=8,'dev'=32] {'grp'}, dimensions={0} | all-to-all | bytes 32768 | tf_op jit(solution)/shard_map/all_to_all | solution.py:17
  536.2 11.9 %all_to_all.215 = f32[32,2,256]{2,1,0:T(2,128)S(1)} all-to-all(f32[32,2,256]{2,1,0:T(2,128)S(1)} %broadcast_in_dim.101), channel_id=1, replica_groups=mesh['grp'=8,'dev'=32] {'dev'}, dimensions={0} | all-to-all | bytes 131072 | tf_op jit(solution)/shard_map/all_to_all | solution.py:17
  (276 shorter events, 54.2 us)
Async XLA Ops:
  0.6 1.3 copy-start.2
  2.0 1.0 copy-start.3
  3.2 1.0 copy-start
  4.2 0.7 copy-start.7
  4.2 0.7 copy-start.8
  5.6 1.0 copy-start.1
  86.6 23.5 %copy-start.5 = (f32[512,256]{0,1:T(8,128)S(1)}, f32[512,256]{0,1:T(8,128)}, u32[]{:S(2)}) copy-start(f32[512,256]{0,1:T(8,128)} %get-tuple-element.121) | copy-start | bytes 1572868
  88.7 19.2 %all-to-all-start.2 = ((f32[256,1,2]{2,1,0:T(1,128)}), f32[256,1,2]{2,1,0:T(1,128)S(1)}, u32[]{:S(2)}, u32[]{:S(2)}) async-start(f32[256,1,2]{2,1,0:T(1,128)} %broadcast_in_dim_broadcast_in_dim_broadcast_in_dim.6), calls=%async_computation.2 | async-start | bytes 262144 | tf_op jit(solution)/shard_map/all_to_all | solution.py:17
  110.9 1.6 copy-start.4
  123.6 12.8 %all-to-all-start.4 = ((f32[32,2,256]{2,1,0:T(2,128)}), f32[32,2,256]{2,1,0:T(2,128)S(1)}, u32[]{:S(2)}, u32[]{:S(2)}) async-start(f32[32,2,256]{2,1,0:T(2,128)} %broadcast_in_dim.71), calls=%async_computation.4 | async-start | bytes 131072 | tf_op jit(solution)/shard_map/all_to_all | solution.py:17
  343.4 22.2 %copy-start.6 = (f32[512,256]{0,1:T(8,128)S(1)}, f32[512,256]{0,1:T(8,128)}, u32[]{:S(2)}) copy-start(f32[512,256]{0,1:T(8,128)} %get-tuple-element.125) | copy-start | bytes 1572868

commit v2 on v1

--- a/solution.py
+++ b/solution.py
@@ -1,11 +1,11 @@
 import jax
 import jax.numpy as jnp
 from jax import lax
-from jax.sharding import PartitionSpec as P
+from jax.sharding import Mesh, PartitionSpec as P
 
 OUTER = 2
 INNER = 8
-AXES = ("grp", "dev")
+AXES = ("x", "core", "z", "y")
 HIGH = lax.Precision.HIGHEST
 
 
@@ -18,24 +18,25 @@
 
 
 def sum_all(value):
-    value = jnp.sum(exchange(value, "grp", lax.axis_size("grp")), 0)
-    return jnp.sum(exchange(value, "dev", lax.axis_size("dev")), 0)
+    value = jnp.sum(exchange(value, ("x", "core"), lax.axis_size(("x", "core"))), 0)
+    return jnp.sum(exchange(value, ("z", "y"), lax.axis_size(("z", "y"))), 0)
 
 
 def sum_columns(first, second, small):
     rank, width = first.shape
-    count = lax.axis_size("grp") * lax.axis_size("dev")
-    share = rank // count
+    plane = ("x", "core", "y")
+    count = lax.axis_size(plane)
     pad = jnp.zeros((rank, 128 - small.shape[0]), jnp.float32)
     packed = jnp.concatenate([first, second, small.T, pad], 1)
     total = packed.shape[1]
-    part = jnp.sum(lax.all_to_all(packed.reshape(count, share, total), AXES, 0, 0), 0)
-    full = exchange(part, AXES, count).reshape(rank, total)
+    part = jnp.sum(lax.all_to_all(packed.reshape(count, rank // count, total), plane, 0, 0), 0)
+    part = jnp.sum(exchange(part, "z", lax.axis_size("z")), 0)
+    full = exchange(part, plane, count).reshape(rank, total)
     return full[:, :width], full[:, width : 2 * width], full[:, 2 * width : 2 * width + small.shape[0]].T
 
 
 def max_all(value):
-    count = lax.axis_size("grp") * lax.axis_size("dev")
+    count = lax.axis_size(AXES)
     return jnp.max(exchange(jnp.broadcast_to(value, (2,)), AXES, count))
 
 
@@ -131,12 +132,13 @@
             scale_right = middle / marg_right
     left = row_left[:, None] * kernel_left * scale_left[None, :]
     right = row_right[:, None] * kernel_right * scale_right[None, :]
-    total_points = left.shape[0] * lax.axis_size("grp") * lax.axis_size("dev")
+    total_points = left.shape[0] * lax.axis_size(AXES)
     factor = float(total_points * rank)
     return (left * factor, right * factor, middle * float(rank))
 
 
 def solution(mesh):
+    mesh = Mesh(mesh.devices.reshape(4, 2, 8, 4), AXES)
     return jax.shard_map(
         local,
         mesh=mesh,

time: 561 us -> 532 us (0.948)
  blocking collectives: 444 us -> 419 us
    all_to_all x2, blocking collectives: 68.3 us -> 38.1 us  [sum_columns(): lax.all_to_all(packed.reshape(count, rank // count, total), plane, 0, 0)]
    all_to_all x32 -> x34, blocking collectives: 376 us -> 381 us  [exchange(): lax.all_to_all(jnp.broadcast_to(value[None], (size,) + value.shape), axes...]
where the time goes in v2:
time: 532 us; the launch traced here: 522 us
  blocking collectives  419 us (79%)
  matrix products  41.7 us (8%)
  waiting for transfers between devices  19.9 us (4%)
  local copies, waits for them, and re-layouts  11.9 us (2%)
  other arithmetic  11.9 us (2%)
  starting transfers between devices  10.5 us (2%)
  between operations  7.2 us (1%)
    all_to_all x34, blocking collectives, exchange(): lax.all_to_all(jnp.broadcast_to(value[None], (size,) + value.shape), axes...  381 us
    all_to_all x2, blocking collectives, sum_columns(): lax.all_to_all(packed.reshape(count, rank // count, total), plane, 0, 0)  38.1 us
    all_to_all x2, waiting for transfers between devices, exchange(): lax.all_to_all(jnp.broadcast_to(value[None], (size,) + value.shape), axes...  19.9 us
  transfers between devices with their start and end apart: 2, of which 2 were waited for; matrix products, arithmetic and copies ran while one was open for 0% of the time, Pallas kernels for 0%

profile of v2, /device:TPU:1, one launch (start us, length us, event | category | flops | bytes accessed | tf_op | source)
XLA Modules:
  0.0 522.3 jit_solution(5196957058632581736)
XLA Ops:
  0.6 1.3 copy.36
  10.6 1.1 copy.37
  11.6 20.8 %all_to_all.192 = f32[32,8,640]{2,1,0:T(8,128)S(1)} all-to-all(f32[32,8,640]{2,1,0:T(8,128)} %bitcast.352), channel_id=1, replica_groups=mesh['x'=4,'core'=2,'z'=8,'y'=4] {'x','core','y'}, dimensions={0} | all-to-all | bytes 1310720 | tf_op jit(solution)/shard_map/all_to_all | solution.py:32
  32.5 16.2 %all_to_all.193 = f32[8,8,640]{2,1,0:T(8,128)S(1)} all-to-all(f32[8,8,640]{2,1,0:T(8,128)S(1)} %broadcast_in_dim.72), channel_id=1, replica_groups=mesh['x'=4,'core'=2,'z'=8,'y'=4] {'z'}, dimensions={0} | all-to-all | bytes 327680 | tf_op jit(solution)/shard_map/all_to_all | solution.py:17
  48.8 18.3 %all_to_all.194 = f32[32,8,640]{2,1,0:T(8,128)S(1)} all-to-all(f32[32,8,640]{2,1,0:T(8,128)S(1)} %broadcast_in_dim.73), channel_id=1, replica_groups=mesh['x'=4,'core'=2,'z'=8,'y'=4] {'x','core','y'}, dimensions={0} | all-to-all | bytes 1310720 | tf_op jit(solution)/shard_map/all_to_all | solution.py:17
  67.5 2.1 abs_reduce_fusion.2
  69.6 2.1 abs_reduce_fusion.3
  73.8 6.1 %all-to-all-start.3 = ((f32[256,1,2]{2,1,0:T(1,128)}), f32[256,1,2]{2,1,0:T(1,128)S(1)}, u32[]{:S(2)}, u32[]{:S(2)}) async-start(f32[256,1,2]{2,1,0:T(1,128)} %broadcast_in_dim_broadcast_in_dim_broadcast_in_dim.6), calls=%async_computation.3 | async-start | bytes 262144 | tf_op jit(solution)/shard_map/all_to_all | solution.py:17
  81.7 11.0 %all-to-all-done.3 = f32[256,1,2]{2,1,0:T(1,128)S(1)} async-done(((f32[256,1,2]{2,1,0:T(1,128)}), f32[256,1,2]{2,1,0:T(1,128)S(1)}, u32[]{:S(2)}, u32[]{:S(2)}) %all-to-all-start.3) | async-done | bytes 2080 | tf_op jit(solution)/shard_map/all_to_all | solution.py:17
  99.6 8.1 %all_to_all.195 = f32[8,2,256]{2,1,0:T(2,128)S(1)} all-to-all(f32[8,2,256]{2,1,0:T(2,128)S(1)} %broadcast_in_dim.75), channel_id=1, replica_groups=mesh['x'=4,'core'=2,'z'=8,'y'=4] {'x','core'}, dimensions={0} | all-to-all | bytes 32768 | tf_op jit(solution)/shard_map/all_to_all | solution.py:17
  108.3 4.3 all-to-all-start.5
  112.7 8.9 %all-to-all-done.5 = f32[32,2,256]{2,1,0:T(2,128)S(1)} async-done(((f32[32,2,256]{2,1,0:T(2,128)}), f32[32,2,256]{2,1,0:T(2,128)S(1)}, u32[]{:S(2)}, u32[]{:S(2)}) %all-to-all-start.5) | async-done | bytes 65568 | tf_op jit(solution)/shard_map/all_to_all | solution.py:17
  123.5 8.9 %all_to_all.196 = f32[8,2,256]{2,1,0:T(2,128)S(1)} all-to-all(f32[8,2,256]{2,1,0:T(2,128)S(1)} %broadcast_in_dim.77), channel_id=1, replica_groups=mesh['x'=4,'core'=2,'z'=8,'y'=4] {'x','core'}, dimensions={0} | all-to-all | bytes 32768 | tf_op jit(solution)/shard_map/all_to_all | solution.py:17
  132.4 11.8 %all_to_all.197 = f32[32,2,256]{2,1,0:T(2,128)S(1)} all-to-all(f32[32,2,256]{2,1,0:T(2,128)S(1)} %broadcast_in_dim.78), channel_id=1, replica_groups=mesh['x'=4,'core'=2,'z'=8,'y'=4] {'z','y'}, dimensions={0} | all-to-all | bytes 131072 | tf_op jit(solution)/shard_map/all_to_all | solution.py:17
  146.2 8.9 %all_to_all.198 = f32[8,2,256]{2,1,0:T(2,128)S(1)} all-to-all(f32[8,2,256]{2,1,0:T(2,128)S(1)} %broadcast_in_dim.79), channel_id=1, replica_groups=mesh['x'=4,'core'=2,'z'=8,'y'=4] {'x','core'}, dimensions={0} | all-to-all | bytes 32768 | tf_op jit(solution)/shard_map/all_to_all | solution.py:17
  155.2 11.9 %all_to_all.199 = f32[32,2,256]{2,1,0:T(2,128)S(1)} all-to-all(f32[32,2,256]{2,1,0:T(2,128)S(1)} %broadcast_in_dim.80), channel_id=1, replica_groups=mesh['x'=4,'core'=2,'z'=8,'y'=4] {'z','y'}, dimensions={0} | all-to-all | bytes 131072 | tf_op jit(solution)/shard_map/all_to_all | solution.py:17
  169.0 8.9 %all_to_all.200 = f32[8,2,256]{2,1,0:T(2,128)S(1)} all-to-all(f32[8,2,256]{2,1,0:T(2,128)S(1)} %broadcast_in_dim.81), channel_id=1, replica_groups=mesh['x'=4,'core'=2,'z'=8,'y'=4] {'x','core'}, dimensions={0} | all-to-all | bytes 32768 | tf_op jit(solution)/shard_map/all_to_all | solution.py:17
  178.0 11.9 %all_to_all.201 = f32[32,2,256]{2,1,0:T(2,128)S(1)} all-to-all(f32[32,2,256]{2,1,0:T(2,128)S(1)} %broadcast_in_dim.82), channel_id=1, replica_groups=mesh['x'=4,'core'=2,'z'=8,'y'=4] {'z','y'}, dimensions={0} | all-to-all | bytes 131072 | tf_op jit(solution)/shard_map/all_to_all | solution.py:17
  191.8 8.9 %all_to_all.202 = f32[8,2,256]{2,1,0:T(2,128)S(1)} all-to-all(f32[8,2,256]{2,1,0:T(2,128)S(1)} %broadcast_in_dim.83), channel_id=1, replica_groups=mesh['x'=4,'core'=2,'z'=8,'y'=4] {'x','core'}, dimensions={0} | all-to-all | bytes 32768 | tf_op jit(solution)/shard_map/all_to_all | solution.py:17
  200.8 11.9 %all_to_all.203 = f32[32,2,256]{2,1,0:T(2,128)S(1)} all-to-all(f32[32,2,256]{2,1,0:T(2,128)S(1)} %broadcast_in_dim.84), channel_id=1, replica_groups=mesh['x'=4,'core'=2,'z'=8,'y'=4] {'z','y'}, dimensions={0} | all-to-all | bytes 131072 | tf_op jit(solution)/shard_map/all_to_all | solution.py:17
  214.6 8.9 %all_to_all.204 = f32[8,2,256]{2,1,0:T(2,128)S(1)} all-to-all(f32[8,2,256]{2,1,0:T(2,128)S(1)} %broadcast_in_dim.85), channel_id=1, replica_groups=mesh['x'=4,'core'=2,'z'=8,'y'=4] {'x','core'}, dimensions={0} | all-to-all | bytes 32768 | tf_op jit(solution)/shard_map/all_to_all | solution.py:17
  223.6 11.9 %all_to_all.205 = f32[32,2,256]{2,1,0:T(2,128)S(1)} all-to-all(f32[32,2,256]{2,1,0:T(2,128)S(1)} %broadcast_in_dim.86), channel_id=1, replica_groups=mesh['x'=4,'core'=2,'z'=8,'y'=4] {'z','y'}, dimensions={0} | all-to-all | bytes 131072 | tf_op jit(solution)/shard_map/all_to_all | solution.py:17
  237.4 8.9 %all_to_all.206 = f32[8,2,256]{2,1,0:T(2,128)S(1)} all-to-all(f32[8,2,256]{2,1,0:T(2,128)S(1)} %broadcast_in_dim.87), channel_id=1, replica_groups=mesh['x'=4,'core'=2,'z'=8,'y'=4] {'x','core'}, dimensions={0} | all-to-all | bytes 32768 | tf_op jit(solution)/shard_map/all_to_all | solution.py:17
  246.4 12.0 %all_to_all.207 = f32[32,2,256]{2,1,0:T(2,128)S(1)} all-to-all(f32[32,2,256]{2,1,0:T(2,128)S(1)} %broadcast_in_dim.88), channel_id=1, replica_groups=mesh['x'=4,'core'=2,'z'=8,'y'=4] {'z','y'}, dimensions={0} | all-to-all | bytes 131072 | tf_op jit(solution)/shard_map/all_to_all | solution.py:17
  258.9 1.0 fusion.10
  260.9 1.0 fusion.14
  263.0 17.2 %all_to_all.208 = f32[32,8,640]{2,1,0:T(8,128)S(1)} all-to-all(f32[32,8,640]{2,1,0:T(8,128)S(1)} %bitcast.353), channel_id=1, replica_groups=mesh['x'=4,'core'=2,'z'=8,'y'=4] {'x','core','y'}, dimensions={0} | all-to-all | bytes 1310720 | tf_op jit(solution)/shard_map/all_to_all | solution.py:32
  280.3 10.5 %all_to_all.209 = f32[8,8,640]{2,1,0:T(8,128)S(1)} all-to-all(f32[8,8,640]{2,1,0:T(8,128)S(1)} %broadcast_in_dim.90), channel_id=1, replica_groups=mesh['x'=4,'core'=2,'z'=8,'y'=4] {'z'}, dimensions={0} | all-to-all | bytes 327680 | tf_op jit(solution)/shard_map/all_to_all | solution.py:17
  290.9 18.5 %all_to_all.210 = f32[32,8,640]{2,1,0:T(8,128)S(1)} all-to-all(f32[32,8,640]{2,1,0:T(8,128)S(1)} %broadcast_in_dim.91), channel_id=1, replica_groups=mesh['x'=4,'core'=2,'z'=8,'y'=4] {'x','core','y'}, dimensions={0} | all-to-all | bytes 1310720 | tf_op jit(solution)/shard_map/all_to_all | solution.py:17
  310.6 1.4 abs_reduce_fusion
  311.9 2.1 abs_reduce_fusion.1
  315.5 18.6 %all_to_all.211 = f32[256,1,2]{2,1,0:T(1,128)S(1)} all-to-all(f32[256,1,2]{2,1,0:T(1,128)S(1)} %broadcast_in_dim_broadcast_in_dim_broadcast_in_dim.7), channel_id=1, replica_groups=mesh['x'=4,'core'=2,'z'=8,'y'=4] {'x','core','z','y'}, dimensions={0} | all-to-all | bytes 4096 | tf_op jit(solution)/shard_map/all_to_all | solution.py:17
  338.4 8.1 %all_to_all.212 = f32[8,2,256]{2,1,0:T(2,128)S(1)} all-to-all(f32[8,2,256]{2,1,0:T(2,128)S(1)} %broadcast_in_dim.92), channel_id=1, replica_groups=mesh['x'=4,'core'=2,'z'=8,'y'=4] {'x','core'}, dimensions={0} | all-to-all | bytes 32768 | tf_op jit(solution)/shard_map/all_to_all | solution.py:17
  346.5 12.2 %all_to_all.213 = f32[32,2,256]{2,1,0:T(2,128)S(1)} all-to-all(f32[32,2,256]{2,1,0:T(2,128)S(1)} %broadcast_in_dim.93), channel_id=1, replica_groups=mesh['x'=4,'core'=2,'z'=8,'y'=4] {'z','y'}, dimensions={0} | all-to-all | bytes 131072 | tf_op jit(solution)/shard_map/all_to_all | solution.py:17
  360.7 9.1 %all_to_all.214 = f32[8,2,256]{2,1,0:T(2,128)S(1)} all-to-all(f32[8,2,256]{2,1,0:T(2,128)S(1)} %broadcast_in_dim.94), channel_id=1, replica_groups=mesh['x'=4,'core'=2,'z'=8,'y'=4] {'x','core'}, dimensions={0} | all-to-all | bytes 32768 | tf_op jit(solution)/shard_map/all_to_all | solution.py:17
  369.9 11.9 %all_to_all.215 = f32[32,2,256]{2,1,0:T(2,128)S(1)} all-to-all(f32[32,2,256]{2,1,0:T(2,128)S(1)} %broadcast_in_dim.95), channel_id=1, replica_groups=mesh['x'=4,'core'=2,'z'=8,'y'=4] {'z','y'}, dimensions={0} | all-to-all | bytes 131072 | tf_op jit(solution)/shard_map/all_to_all | solution.py:17
  383.8 8.9 %all_to_all.216 = f32[8,2,256]{2,1,0:T(2,128)S(1)} all-to-all(f32[8,2,256]{2,1,0:T(2,128)S(1)} %broadcast_in_dim.96), channel_id=1, replica_groups=mesh['x'=4,'core'=2,'z'=8,'y'=4] {'x','core'}, dimensions={0} | all-to-all | bytes 32768 | tf_op jit(solution)/shard_map/all_to_all | solution.py:17
  392.7 11.9 %all_to_all.217 = f32[32,2,256]{2,1,0:T(2,128)S(1)} all-to-all(f32[32,2,256]{2,1,0:T(2,128)S(1)} %broadcast_in_dim.97), channel_id=1, replica_groups=mesh['x'=4,'core'=2,'z'=8,'y'=4] {'z','y'}, dimensions={0} | all-to-all | bytes 131072 | tf_op jit(solution)/shard_map/all_to_all | solution.py:17
  406.6 8.9 %all_to_all.218 = f32[8,2,256]{2,1,0:T(2,128)S(1)} all-to-all(f32[8,2,256]{2,1,0:T(2,128)S(1)} %broadcast_in_dim.98), channel_id=1, replica_groups=mesh['x'=4,'core'=2,'z'=8,'y'=4] {'x','core'}, dimensions={0} | all-to-all | bytes 32768 | tf_op jit(solution)/shard_map/all_to_all | solution.py:17
  415.5 11.9 %all_to_all.219 = f32[32,2,256]{2,1,0:T(2,128)S(1)} all-to-all(f32[32,2,256]{2,1,0:T(2,128)S(1)} %broadcast_in_dim.99), channel_id=1, replica_groups=mesh['x'=4,'core'=2,'z'=8,'y'=4] {'z','y'}, dimensions={0} | all-to-all | bytes 131072 | tf_op jit(solution)/shard_map/all_to_all | solution.py:17
  429.4 8.9 %all_to_all.220 = f32[8,2,256]{2,1,0:T(2,128)S(1)} all-to-all(f32[8,2,256]{2,1,0:T(2,128)S(1)} %broadcast_in_dim.100), channel_id=1, replica_groups=mesh['x'=4,'core'=2,'z'=8,'y'=4] {'x','core'}, dimensions={0} | all-to-all | bytes 32768 | tf_op jit(solution)/shard_map/all_to_all | solution.py:17
  438.3 11.9 %all_to_all.221 = f32[32,2,256]{2,1,0:T(2,128)S(1)} all-to-all(f32[32,2,256]{2,1,0:T(2,128)S(1)} %broadcast_in_dim.101), channel_id=1, replica_groups=mesh['x'=4,'core'=2,'z'=8,'y'=4] {'z','y'}, dimensions={0} | all-to-all | bytes 131072 | tf_op jit(solution)/shard_map/all_to_all | solution.py:17
  452.2 8.9 %all_to_all.222 = f32[8,2,256]{2,1,0:T(2,128)S(1)} all-to-all(f32[8,2,256]{2,1,0:T(2,128)S(1)} %broadcast_in_dim.102), channel_id=1, replica_groups=mesh['x'=4,'core'=2,'z'=8,'y'=4] {'x','core'}, dimensions={0} | all-to-all | bytes 32768 | tf_op jit(solution)/shard_map/all_to_all | solution.py:17
  461.1 11.9 %all_to_all.223 = f32[32,2,256]{2,1,0:T(2,128)S(1)} all-to-all(f32[32,2,256]{2,1,0:T(2,128)S(1)} %broadcast_in_dim.103), channel_id=1, replica_groups=mesh['x'=4,'core'=2,'z'=8,'y'=4] {'z','y'}, dimensions={0} | all-to-all | bytes 131072 | tf_op jit(solution)/shard_map/all_to_all | solution.py:17
  475.0 8.9 %all_to_all.224 = f32[8,2,256]{2,1,0:T(2,128)S(1)} all-to-all(f32[8,2,256]{2,1,0:T(2,128)S(1)} %broadcast_in_dim.104), channel_id=1, replica_groups=mesh['x'=4,'core'=2,'z'=8,'y'=4] {'x','core'}, dimensions={0} | all-to-all | bytes 32768 | tf_op jit(solution)/shard_map/all_to_all | solution.py:17
  484.0 12.1 %all_to_all.225 = f32[32,2,256]{2,1,0:T(2,128)S(1)} all-to-all(f32[32,2,256]{2,1,0:T(2,128)S(1)} %broadcast_in_dim.105), channel_id=1, replica_groups=mesh['x'=4,'core'=2,'z'=8,'y'=4] {'z','y'}, dimensions={0} | all-to-all | bytes 131072 | tf_op jit(solution)/shard_map/all_to_all | solution.py:17
  498.0 8.9 %all_to_all.226 = f32[8,2,256]{2,1,0:T(2,128)S(1)} all-to-all(f32[8,2,256]{2,1,0:T(2,128)S(1)} %broadcast_in_dim.106), channel_id=1, replica_groups=mesh['x'=4,'core'=2,'z'=8,'y'=4] {'x','core'}, dimensions={0} | all-to-all | bytes 32768 | tf_op jit(solution)/shard_map/all_to_all | solution.py:17
  506.9 11.8 %all_to_all.227 = f32[32,2,256]{2,1,0:T(2,128)S(1)} all-to-all(f32[32,2,256]{2,1,0:T(2,128)S(1)} %broadcast_in_dim.107), channel_id=1, replica_groups=mesh['x'=4,'core'=2,'z'=8,'y'=4] {'z','y'}, dimensions={0} | all-to-all | bytes 131072 | tf_op jit(solution)/shard_map/all_to_all | solution.py:17
  (282 shorter events, 53.6 us)
Async XLA Ops:
  0.6 1.3 copy-start.2
  2.0 1.0 copy-start.3
  3.2 1.0 copy-start
  4.2 0.7 copy-start.7
  4.2 0.7 copy-start.8
  5.6 1.0 copy-start.1
  71.7 23.1 %copy-start.5 = (f32[512,256]{0,1:T(8,128)S(1)}, f32[512,256]{0,1:T(8,128)}, u32[]{:S(2)}) copy-start(f32[512,256]{0,1:T(8,128)} %get-tuple-element.121) | copy-start | bytes 1572868
  73.8 18.9 %all-to-all-start.3 = ((f32[256,1,2]{2,1,0:T(1,128)}), f32[256,1,2]{2,1,0:T(1,128)S(1)}, u32[]{:S(2)}, u32[]{:S(2)}) async-start(f32[256,1,2]{2,1,0:T(1,128)} %broadcast_in_dim_broadcast_in_dim_broadcast_in_dim.6), calls=%async_computation.3 | async-start | bytes 262144 | tf_op jit(solution)/shard_map/all_to_all | solution.py:17
  95.6 1.6 copy-start.4
  108.3 13.2 %all-to-all-start.5 = ((f32[32,2,256]{2,1,0:T(2,128)}), f32[32,2,256]{2,1,0:T(2,128)S(1)}, u32[]{:S(2)}, u32[]{:S(2)}) async-start(f32[32,2,256]{2,1,0:T(2,128)} %broadcast_in_dim.76), calls=%async_computation.5 | async-start | bytes 131072 | tf_op jit(solution)/shard_map/all_to_all | solution.py:17
  314.0 22.2 %copy-start.6 = (f32[512,256]{0,1:T(8,128)S(1)}, f32[512,256]{0,1:T(8,128)}, u32[]{:S(2)}) copy-start(f32[512,256]{0,1:T(8,128)} %get-tuple-element.125) | copy-start | bytes 1572868

commit v3 on v0

v3 whole, which is shorter than its diff:
```python
import jax
import jax.numpy as jnp
from jax import lax
from jax.experimental import pallas as pl
from jax.experimental.pallas import tpu as pltpu
from jax.sharding import Mesh, PartitionSpec as P

OUTER = 2
INNER = 8
LANES = 128
AXES = ("x", "core", "z", "y")
PLANE = ("x", "core", "y")
HIGH = lax.Precision.HIGHEST
F32 = jnp.float32


def chunks(n):
    return [slice(j, j + LANES) for j in range(0, n, LANES)]


def column(row):
    return jnp.transpose(jnp.broadcast_to(row, (LANES, row.shape[1])))


def row_of(partial):
    return jnp.sum(jnp.transpose(partial), 0, keepdims=True)


def widen(col, n):
    return jnp.concatenate([col] * (n // LANES), 1)


def pack(weights, embeds, norms, packed_ref, extra):
    rank, width = packed_ref.shape[0], embeds[0].shape[1]
    lane = lax.broadcasted_iota(jnp.int32, (rank, LANES), 1)
    small = jnp.zeros((rank, LANES), F32)
    for s in range(2):
        w = weights[s]
        packed_ref[:, s * width : (s + 1) * width] = jnp.dot(w, embeds[s], precision=HIGH, preferred_element_type=F32)
        small = jnp.where(lane == 2 * s, jnp.sum(w * norms[s], 1, keepdims=True), small)
        small = jnp.where(lane == 2 * s + 1, jnp.sum(w, 1, keepdims=True), small)
    for n, value in enumerate(extra):
        small = jnp.where(lane == 4 + n, value, small)
    packed_ref[:, 2 * width :] = small


def begin_kernel(x_ref, y_ref, a_ref, b_ref, mass_ref, w1_ref, w2_ref, norm_ref, packed_ref):
    embeds, weights, norms, totals = [], [], [], []
    for s, (e_ref, f_ref, w_ref) in enumerate(((x_ref, a_ref, w1_ref), (y_ref, b_ref, w2_ref))):
        factor = jnp.transpose(f_ref[...])
        mass = mass_ref[s : s + 1, :]
        w_ref[...] = factor * (mass / jnp.sum(factor, 0, keepdims=True))
        e = e_ref[...]
        ones = jnp.ones((8, e.shape[1]), F32)
        norm = lax.dot_general(ones, e * e, (((1,), (1,)), ((), ())), precision=HIGH, preferred_element_type=F32)[:1]
        norm_ref[s : s + 1, :] = norm
        embeds.append(e)
        weights.append(w_ref[...])
        norms.append(norm)
        totals.append(jnp.sum(mass, 1, keepdims=True))
    pack(weights, embeds, norms, packed_ref, totals)


def gradients(full_ref, embeds, norm_ref, inverse, middle, grad_refs, peak_ref):
    rank, width = full_ref.shape[0], embeds[0].shape[1]
    small = full_ref[:, 2 * width :]
    cross = [full_ref[:, s * width : (s + 1) * width] * widen(inverse[s], width) for s in range(2)]
    heavy = [small[:, 2 * s : 2 * s + 1] * inverse[s] for s in range(2)]
    plain = [small[:, 2 * s + 1 : 2 * s + 2] * inverse[s] for s in range(2)]
    diagonal = heavy[0] * plain[1] + plain[0] * heavy[1] - 2.0 * jnp.sum(cross[0] * cross[1], 1, keepdims=True)
    grad_middle = -diagonal / (middle * middle)
    over = 1.0 / middle
    peak = jnp.max(jnp.abs(grad_middle), 0, keepdims=True)
    for s in range(2):
        product = lax.dot_general(
            cross[1 - s] * widen(-2.0 * over, width),
            embeds[s],
            (((1,), (1,)), ((), ())),
            precision=HIGH,
            preferred_element_type=F32,
        )
        points = product.shape[1]
        norm = norm_ref[s : s + 1, :]
        grad = product + widen(plain[1 - s] * over, points) * norm + widen(heavy[1 - s] * over, points)
        grad_refs[s][...] = grad
        for c in chunks(points):
            peak = jnp.maximum(peak, jnp.max(jnp.abs(grad[:, c]), 0, keepdims=True))
    peak_ref[...] = jnp.broadcast_to(jnp.max(peak, 1, keepdims=True), peak_ref.shape)
    return grad_middle


def rows(columns):
    n = columns[0].shape[0]
    lane = lax.broadcasted_iota(jnp.int32, (n, LANES), 1)
    block = jnp.zeros((n, LANES), F32)
    for i, c in enumerate(columns):
        block = jnp.where(lane == i, c, block)
    return jnp.transpose(block)[:8]


def first_gradients_kernel(full_ref, x_ref, y_ref, norm_ref, mass_ref, g1_ref, g2_ref, peak_ref, rows_ref, share_ref):
    rank = full_ref.shape[0]
    width = x_ref.shape[1]
    inverse = [
        1.0 / jnp.broadcast_to(full_ref[:, 2 * width + 4 + s : 2 * width + 5 + s], (rank, LANES)) for s in range(2)
    ]
    for s in range(2):
        mass = mass_ref[s : s + 1, :]
        share_ref[s : s + 1, :] = mass * widen(inverse[s][:1], mass.shape[1])
    middle = jnp.full((rank, LANES), 1.0 / rank, F32)
    grad_middle = gradients(
        full_ref, (x_ref[...], y_ref[...]), norm_ref, inverse, middle, (g1_ref, g2_ref), peak_ref
    )
    rows_ref[...] = rows([middle, grad_middle, inverse[0], inverse[1]])


def next_gradients_kernel(full_ref, x_ref, y_ref, norm_ref, scale_ref, kmid_ref, g1_ref, g2_ref, peak_ref, rows_ref):
    rank = full_ref.shape[0]
    width = x_ref.shape[1]
    marg = [
        jnp.broadcast_to(full_ref[:, 2 * width + 2 * s + 1 : 2 * width + 2 * s + 2], (rank, LANES)) for s in range(2)
    ]
    scale = [column(scale_ref[s : s + 1, :]) for s in range(2)]
    cubed = column(kmid_ref[...]) * scale[0] * marg[0] * scale[1] * marg[1]
    middle = jnp.exp(jnp.log(cubed) * (1.0 / 3.0))
    inverse = [middle / marg[s] for s in range(2)]
    grad_middle = gradients(
        full_ref, (x_ref[...], y_ref[...]), norm_ref, inverse, middle, (g1_ref, g2_ref), peak_ref
    )
    rows_ref[...] = rows([middle, grad_middle, inverse[0], inverse[1]])


def scaling(k_ref, share, scale):
    partial = jnp.zeros((k_ref.shape[0], LANES), F32)
    factors = []
    for c in chunks(k_ref.shape[1]):
        k = k_ref[:, c]
        total = jnp.sum(k if scale is None else k * scale, 0, keepdims=True)
        factor = share[:, c] / total
        partial = partial + k * factor
        factors.append(factor)
    return jnp.concatenate(factors, 1), row_of(partial)


def first_step_kernel(g1_ref, g2_ref, w1_ref, w2_ref, peak_ref, rows_ref, share_ref, k1_ref, k2_ref, kmid_ref, sums_ref):
    middle, grad_middle = rows_ref[0:1, :], rows_ref[1:2, :]
    peak = jnp.max(peak_ref[...], 1, keepdims=True)
    rate = 30.0 / (peak * peak + 1e-06)
    kmid_ref[...] = middle * jnp.exp(-rate * grad_middle)
    for s, (g_ref, w_ref, k_ref) in enumerate(((g1_ref, w1_ref, k1_ref), (g2_ref, w2_ref, k2_ref))):
        inverse = column(rows_ref[2 + s : 3 + s, :])
        for c in chunks(k_ref.shape[1]):
            k_ref[:, c] = (w_ref[:, c] * inverse) * jnp.exp(-rate * g_ref[:, c])
        _, sums_ref[s : s + 1, :] = scaling(k_ref, share_ref[s : s + 1, :], None)


def step_kernel(k1_ref, k2_ref, share_ref, scale_ref, sums_ref, *factor_ref):
    for s, k_ref in enumerate((k1_ref, k2_ref)):
        factor, sums_ref[s : s + 1, :] = scaling(
            k_ref, share_ref[s : s + 1, :], column(scale_ref[s : s + 1, :])
        )
        for ref in factor_ref:
            ref[s : s + 1, :] = factor


def last_step_kernel(k1_ref, k2_ref, share_ref, scale_ref, x_ref, y_ref, norm_ref, w1_ref, w2_ref, packed_ref):
    for s, (k_ref, w_ref) in enumerate(((k1_ref, w1_ref), (k2_ref, w2_ref))):
        scale = column(scale_ref[s : s + 1, :])
        for c in chunks(k_ref.shape[1]):
            k = k_ref[:, c]
            w_ref[:, c] = k * (share_ref[s : s + 1, c] / jnp.sum(k * scale, 0, keepdims=True))
    norms = [norm_ref[s : s + 1, :] for s in range(2)]
    pack((w1_ref[...], w2_ref[...]), (x_ref[...], y_ref[...]), norms, packed_ref, [])


def end_kernel(total, k1_ref, k2_ref, factor_ref, scale_ref, o1_ref, o2_ref):
    for s, (k_ref, o_ref) in enumerate(((k1_ref, o1_ref), (k2_ref, o2_ref))):
        scale = column(scale_ref[s : s + 1, :])
        for c in chunks(k_ref.shape[1]):
            value = (k_ref[:, c] * factor_ref[s : s + 1, c]) * scale * total
            o_ref[c, :] = jnp.transpose(value)


def in_vmem(shape):
    return pltpu.VMEM(shape, F32)


def to_vmem(array):
    return pltpu.with_memory_space_constraint(array, pltpu.VMEM)


def call(kernel, outs, *args):
    return pl.pallas_call(
        kernel, out_shape=outs, compiler_params=pltpu.CompilerParams(vmem_limit_bytes=32 * 2**20)
    )(*[to_vmem(a) for a in args])


def exchange(value, axes):
    return lax.all_to_all(jnp.broadcast_to(value[None], (lax.axis_size(axes),) + value.shape), axes, 0, 0)


def sum_all(value):
    value = jnp.sum(exchange(value, ("x", "core")), 0)
    return jnp.sum(exchange(value, ("z", "y")), 0)


def sum_columns(packed):
    rank, total = packed.shape
    count = lax.axis_size(PLANE)
    part = jnp.sum(lax.all_to_all(packed.reshape(count, rank // count, total), PLANE, 0, 0), 0)
    part = jnp.sum(exchange(part, "z"), 0)
    return exchange(part, PLANE).reshape(rank, total)


def max_all(value):
    return jnp.max(exchange(value, AXES), 0)


def local(embed_source, embed_target, mass_source, mass_target, start_source, start_target):
    points, rank = start_source.shape
    width = embed_source.shape[1]
    embeds = (embed_source, embed_target)
    tall, line, top, pair = in_vmem((rank, points)), in_vmem((8, rank)), in_vmem((1, LANES)), in_vmem((2, points))
    sums_of, packed_of = in_vmem((2, rank)), in_vmem((rank, 2 * width + LANES))
    mass = jnp.stack([mass_source, mass_target])
    w1, w2, norm, packed = call(
        begin_kernel, [tall, tall, pair, packed_of], *embeds, start_source, start_target, mass
    )
    for outer in range(OUTER):
        full = sum_columns(packed)
        if outer == 0:
            g1, g2, peak, small, share = call(
                first_gradients_kernel, [tall, tall, top, line, pair], full, *embeds, norm, mass
            )
        else:
            g1, g2, peak, small = call(
                next_gradients_kernel, [tall, tall, top, line], full, *embeds, norm, scale, kmid
            )
        k1, k2, kmid, sums = call(
            first_step_kernel, [tall, tall, in_vmem((1, rank)), sums_of], g1, g2, w1, w2, max_all(peak), small, share
        )
        scale = jnp.ones((2, rank), F32)
        for inner in range(INNER):
            if inner == INNER - 1 and outer < OUTER - 1:
                w1, w2, packed = call(
                    last_step_kernel, [tall, tall, packed_of], k1, k2, share, scale, *embeds, norm
                )
                break
            if inner == INNER - 1:
                sums, factor = call(step_kernel, [sums_of, pair], k1, k2, share, scale)
            elif inner > 0:
                (sums,) = call(step_kernel, [sums_of], k1, k2, share, scale)
            margins = sum_all(sums)
            middle = jnp.cbrt(kmid * scale[:1] * margins[:1] * scale[1:] * margins[1:])
            scale = middle / margins
    total = float(points * lax.axis_size(AXES) * rank)
    result = jax.ShapeDtypeStruct((points, rank), F32)
    left, right = call(lambda *refs: end_kernel(total, *refs), [result, result], k1, k2, factor, scale)
    return left, right, middle[0] * float(rank)


def solution(mesh):
    mesh = Mesh(mesh.devices.reshape(4, 2, 8, 4), AXES)
    return jax.shard_map(
        local,
        mesh=mesh,
        in_specs=(P(AXES, None), P(AXES, None), P(AXES), P(AXES), P(AXES, None), P(AXES, None)),
        out_specs=(P(AXES, None), P(AXES, None), P()),
        check_vma=False,
    )
```

time: 2170 us -> 481 us (0.22)
  blocking collectives: 1710 us -> 450 us
  waiting for transfers between devices: 344 us -> 0 us
  matrix products: 41.9 us -> 0 us
  other arithmetic: 31 us -> 2.93 us
    psum x21 -> x0, blocking collectives: 1560 us -> none  [the longest x16 1180 us: local(): lax.psum(jnp.stack([jnp.dot(row_left, kernel_left, precision=HIGH), jnp.d...]
    all_to_all x0 -> x38, blocking collectives: none -> 450 us  [the longest x36 412 us: exchange(): lax.all_to_all(jnp.broadcast_to(value[None], (lax.axis_size(axes),) + val...]
    psum x2 -> x0, waiting for transfers between devices: 344 us -> none  [reduce_factors(): summed = lax.psum((big, small), ('grp', 'dev'))]
    pmax x2 -> x0, blocking collectives: 155 us -> none  [local(): lax.pmax((jnp.max(jnp.abs(grad_left)), jnp.max(jnp.abs(grad_right))), ('g...]
    dot_general x76 -> x0, matrix products: 41.9 us -> none  [the longest x16 8.14 us: local(): jnp.dot(row_right, kernel_right, precision=HIGH)]
    div x52 -> x15, other arithmetic: 22.8 us -> 0.09 us  [local(): scale = middle / margins]
  transfers between devices with their start and end apart: 2 -> 0, of which waited for: 2 -> 0; matrix products, arithmetic and copies ran while one was open for 0% -> 0% of each run, Pallas kernels for 0% -> 0%
where the time goes in v3:
time: 481 us; the launch traced here: 479 us
  blocking collectives  450 us (94%)
  Pallas kernels  13.3 us (3%)
  local copies, waits for them, and re-layouts  11.9 us (2%)
    all_to_all x36, blocking collectives, exchange(): lax.all_to_all(jnp.broadcast_to(value[None], (lax.axis_size(axes),) + val...  412 us
    all_to_all x2, blocking collectives, sum_columns(): lax.all_to_all(packed.reshape(count, rank // count, total), PLANE, 0, 0)  38 us
    pallas_call x20, Pallas kernels, call(): pl.pallas_call(kernel, out_shape=outs, compiler_params=pltpu.CompilerPara...  13.3 us
    unnamed x30, local copies, waits for them, and re-layouts  11.2 us

profile of v3, /device:TPU:1, one launch (start us, length us, event | category | flops | bytes accessed | tf_op | source)
XLA Modules:
  0.0 479.4 jit_solution(12678853603134818912)
XLA Ops:
  3.0 1.0 copy-done.2
  4.1 1.0 copy-done.12
  5.1 1.0 copy-done.13
  6.2 2.1 shard_map.85
  8.3 20.6 %all_to_all.190 = f32[32,8,640]{2,1,0:T(8,128)S(1)} all-to-all(f32[32,8,640]{2,1,0:T(8,128)S(1)} %bitcast.30), channel_id=1, replica_groups=mesh['x'=4,'core'=2,'z'=8,'y'=4] {'x','core','y'}, dimensions={0} | all-to-all | bytes 1310720 | tf_op jit(solution)/shard_map/all_to_all | solution.py:210
  28.9 16.2 %all_to_all.191 = f32[8,8,640]{2,1,0:T(8,128)S(1)} all-to-all(f32[8,8,640]{2,1,0:T(8,128)S(1)} %broadcast_in_dim.76), channel_id=1, replica_groups=mesh['x'=4,'core'=2,'z'=8,'y'=4] {'z'}, dimensions={0} | all-to-all | bytes 327680 | tf_op jit(solution)/shard_map/all_to_all | solution.py:199
  45.3 18.5 %all_to_all.192 = f32[32,8,640]{2,1,0:T(8,128)S(1)} all-to-all(f32[32,8,640]{2,1,0:T(8,128)S(1)} %broadcast_in_dim.77), channel_id=1, replica_groups=mesh['x'=4,'core'=2,'z'=8,'y'=4] {'x','core','y'}, dimensions={0} | all-to-all | bytes 1310720 | tf_op jit(solution)/shard_map/all_to_all | solution.py:199
  63.7 1.4 shard_map.86
  66.8 18.5 %all_to_all.193 = f32[256,1,128]{2,1,0:T(1,128)S(1)} all-to-all(f32[256,1,128]{2,1,0:T(1,128)S(1)} %broadcast_in_dim.79), channel_id=1, replica_groups=mesh['x'=4,'core'=2,'z'=8,'y'=4] {'x','core','z','y'}, dimensions={0} | all-to-all | bytes 262144 | tf_op jit(solution)/shard_map/all_to_all | solution.py:199
  85.4 1.0 copy-done.9
  86.4 1.0 copy-done.11
  88.0 8.1 %all_to_all.194 = f32[8,2,256]{2,1,0:T(2,128)S(1)} all-to-all(f32[8,2,256]{2,1,0:T(2,128)S(1)} %broadcast_in_dim.80), channel_id=1, replica_groups=mesh['x'=4,'core'=2,'z'=8,'y'=4] {'x','core'}, dimensions={0} | all-to-all | bytes 32768 | tf_op jit(solution)/shard_map/all_to_all | solution.py:199
  96.1 12.0 %all_to_all.195 = f32[32,2,256]{2,1,0:T(2,128)S(1)} all-to-all(f32[32,2,256]{2,1,0:T(2,128)S(1)} %broadcast_in_dim.81), channel_id=1, replica_groups=mesh['x'=4,'core'=2,'z'=8,'y'=4] {'z','y'}, dimensions={0} | all-to-all | bytes 131072 | tf_op jit(solution)/shard_map/all_to_all | solution.py:199
  108.5 9.1 %all_to_all.196 = f32[8,2,256]{2,1,0:T(2,128)S(1)} all-to-all(f32[8,2,256]{2,1,0:T(2,128)S(1)} %broadcast_in_dim.82), channel_id=1, replica_groups=mesh['x'=4,'core'=2,'z'=8,'y'=4] {'x','core'}, dimensions={0} | all-to-all | bytes 32768 | tf_op jit(solution)/shard_map/all_to_all | solution.py:199
  117.7 11.9 %all_to_all.197 = f32[32,2,256]{2,1,0:T(2,128)S(1)} all-to-all(f32[32,2,256]{2,1,0:T(2,128)S(1)} %broadcast_in_dim.83), channel_id=1, replica_groups=mesh['x'=4,'core'=2,'z'=8,'y'=4] {'z','y'}, dimensions={0} | all-to-all | bytes 131072 | tf_op jit(solution)/shard_map/all_to_all | solution.py:199
  130.1 8.9 %all_to_all.198 = f32[8,2,256]{2,1,0:T(2,128)S(1)} all-to-all(f32[8,2,256]{2,1,0:T(2,128)S(1)} %broadcast_in_dim.84), channel_id=1, replica_groups=mesh['x'=4,'core'=2,'z'=8,'y'=4] {'x','core'}, dimensions={0} | all-to-all | bytes 32768 | tf_op jit(solution)/shard_map/all_to_all | solution.py:199
  139.0 11.9 %all_to_all.199 = f32[32,2,256]{2,1,0:T(2,128)S(1)} all-to-all(f32[32,2,256]{2,1,0:T(2,128)S(1)} %broadcast_in_dim.85), channel_id=1, replica_groups=mesh['x'=4,'core'=2,'z'=8,'y'=4] {'z','y'}, dimensions={0} | all-to-all | bytes 131072 | tf_op jit(solution)/shard_map/all_to_all | solution.py:199
  151.4 8.9 %all_to_all.200 = f32[8,2,256]{2,1,0:T(2,128)S(1)} all-to-all(f32[8,2,256]{2,1,0:T(2,128)S(1)} %broadcast_in_dim.86), channel_id=1, replica_groups=mesh['x'=4,'core'=2,'z'=8,'y'=4] {'x','core'}, dimensions={0} | all-to-all | bytes 32768 | tf_op jit(solution)/shard_map/all_to_all | solution.py:199
  160.3 11.9 %all_to_all.201 = f32[32,2,256]{2,1,0:T(2,128)S(1)} all-to-all(f32[32,2,256]{2,1,0:T(2,128)S(1)} %broadcast_in_dim.87), channel_id=1, replica_groups=mesh['x'=4,'core'=2,'z'=8,'y'=4] {'z','y'}, dimensions={0} | all-to-all | bytes 131072 | tf_op jit(solution)/shard_map/all_to_all | solution.py:199
  172.7 8.9 %all_to_all.202 = f32[8,2,256]{2,1,0:T(2,128)S(1)} all-to-all(f32[8,2,256]{2,1,0:T(2,128)S(1)} %broadcast_in_dim.88), channel_id=1, replica_groups=mesh['x'=4,'core'=2,'z'=8,'y'=4] {'x','core'}, dimensions={0} | all-to-all | bytes 32768 | tf_op jit(solution)/shard_map/all_to_all | solution.py:199
  181.6 11.9 %all_to_all.203 = f32[32,2,256]{2,1,0:T(2,128)S(1)} all-to-all(f32[32,2,256]{2,1,0:T(2,128)S(1)} %broadcast_in_dim.89), channel_id=1, replica_groups=mesh['x'=4,'core'=2,'z'=8,'y'=4] {'z','y'}, dimensions={0} | all-to-all | bytes 131072 | tf_op jit(solution)/shard_map/all_to_all | solution.py:199
  194.0 8.9 %all_to_all.204 = f32[8,2,256]{2,1,0:T(2,128)S(1)} all-to-all(f32[8,2,256]{2,1,0:T(2,128)S(1)} %broadcast_in_dim.90), channel_id=1, replica_groups=mesh['x'=4,'core'=2,'z'=8,'y'=4] {'x','core'}, dimensions={0} | all-to-all | bytes 32768 | tf_op jit(solution)/shard_map/all_to_all | solution.py:199
  202.9 12.0 %all_to_all.205 = f32[32,2,256]{2,1,0:T(2,128)S(1)} all-to-all(f32[32,2,256]{2,1,0:T(2,128)S(1)} %broadcast_in_dim.91), channel_id=1, replica_groups=mesh['x'=4,'core'=2,'z'=8,'y'=4] {'z','y'}, dimensions={0} | all-to-all | bytes 131072 | tf_op jit(solution)/shard_map/all_to_all | solution.py:199
  215.4 8.8 %all_to_all.206 = f32[8,2,256]{2,1,0:T(2,128)S(1)} all-to-all(f32[8,2,256]{2,1,0:T(2,128)S(1)} %broadcast_in_dim.92), channel_id=1, replica_groups=mesh['x'=4,'core'=2,'z'=8,'y'=4] {'x','core'}, dimensions={0} | all-to-all | bytes 32768 | tf_op jit(solution)/shard_map/all_to_all | solution.py:199
  224.2 11.9 %all_to_all.207 = f32[32,2,256]{2,1,0:T(2,128)S(1)} all-to-all(f32[32,2,256]{2,1,0:T(2,128)S(1)} %broadcast_in_dim.93), channel_id=1, replica_groups=mesh['x'=4,'core'=2,'z'=8,'y'=4] {'z','y'}, dimensions={0} | all-to-all | bytes 131072 | tf_op jit(solution)/shard_map/all_to_all | solution.py:199
  236.2 1.5 shard_map.94
  237.8 17.4 %all_to_all.208 = f32[32,8,640]{2,1,0:T(8,128)S(1)} all-to-all(f32[32,8,640]{2,1,0:T(8,128)S(1)} %bitcast.29), channel_id=1, replica_groups=mesh['x'=4,'core'=2,'z'=8,'y'=4] {'x','core','y'}, dimensions={0} | all-to-all | bytes 1310720 | tf_op jit(solution)/shard_map/all_to_all | solution.py:210
  255.2 10.5 %all_to_all.209 = f32[8,8,640]{2,1,0:T(8,128)S(1)} all-to-all(f32[8,8,640]{2,1,0:T(8,128)S(1)} %broadcast_in_dim.94), channel_id=1, replica_groups=mesh['x'=4,'core'=2,'z'=8,'y'=4] {'z'}, dimensions={0} | all-to-all | bytes 327680 | tf_op jit(solution)/shard_map/all_to_all | solution.py:199
  265.7 18.5 %all_to_all.210 = f32[32,8,640]{2,1,0:T(8,128)S(1)} all-to-all(f32[32,8,640]{2,1,0:T(8,128)S(1)} %broadcast_in_dim.95), channel_id=1, replica_groups=mesh['x'=4,'core'=2,'z'=8,'y'=4] {'x','core','y'}, dimensions={0} | all-to-all | bytes 1310720 | tf_op jit(solution)/shard_map/all_to_all | solution.py:199
  284.2 1.5 shard_map.95
  287.4 18.7 %all_to_all.211 = f32[256,1,128]{2,1,0:T(1,128)S(1)} all-to-all(f32[256,1,128]{2,1,0:T(1,128)S(1)} %broadcast_in_dim.97), channel_id=1, replica_groups=mesh['x'=4,'core'=2,'z'=8,'y'=4] {'x','core','z','y'}, dimensions={0} | all-to-all | bytes 262144 | tf_op jit(solution)/shard_map/all_to_all | solution.py:199
  307.7 8.1 %all_to_all.212 = f32[8,2,256]{2,1,0:T(2,128)S(1)} all-to-all(f32[8,2,256]{2,1,0:T(2,128)S(1)} %broadcast_in_dim.98), channel_id=1, replica_groups=mesh['x'=4,'core'=2,'z'=8,'y'=4] {'x','core'}, dimensions={0} | all-to-all | bytes 32768 | tf_op jit(solution)/shard_map/all_to_all | solution.py:199
  315.8 12.0 %all_to_all.213 = f32[32,2,256]{2,1,0:T(2,128)S(1)} all-to-all(f32[32,2,256]{2,1,0:T(2,128)S(1)} %broadcast_in_dim.99), channel_id=1, replica_groups=mesh['x'=4,'core'=2,'z'=8,'y'=4] {'z','y'}, dimensions={0} | all-to-all | bytes 131072 | tf_op jit(solution)/shard_map/all_to_all | solution.py:199
  328.3 9.1 %all_to_all.214 = f32[8,2,256]{2,1,0:T(2,128)S(1)} all-to-all(f32[8,2,256]{2,1,0:T(2,128)S(1)} %broadcast_in_dim.100), channel_id=1, replica_groups=mesh['x'=4,'core'=2,'z'=8,'y'=4] {'x','core'}, dimensions={0} | all-to-all | bytes 32768 | tf_op jit(solution)/shard_map/all_to_all | solution.py:199
  337.5 11.9 %all_to_all.215 = f32[32,2,256]{2,1,0:T(2,128)S(1)} all-to-all(f32[32,2,256]{2,1,0:T(2,128)S(1)} %broadcast_in_dim.101), channel_id=1, replica_groups=mesh['x'=4,'core'=2,'z'=8,'y'=4] {'z','y'}, dimensions={0} | all-to-all | bytes 131072 | tf_op jit(solution)/shard_map/all_to_all | solution.py:199
  349.8 8.9 %all_to_all.216 = f32[8,2,256]{2,1,0:T(2,128)S(1)} all-to-all(f32[8,2,256]{2,1,0:T(2,128)S(1)} %broadcast_in_dim.102), channel_id=1, replica_groups=mesh['x'=4,'core'=2,'z'=8,'y'=4] {'x','core'}, dimensions={0} | all-to-all | bytes 32768 | tf_op jit(solution)/shard_map/all_to_all | solution.py:199
  358.8 11.9 %all_to_all.217 = f32[32,2,256]{2,1,0:T(2,128)S(1)} all-to-all(f32[32,2,256]{2,1,0:T(2,128)S(1)} %broadcast_in_dim.103), channel_id=1, replica_groups=mesh['x'=4,'core'=2,'z'=8,'y'=4] {'z','y'}, dimensions={0} | all-to-all | bytes 131072 | tf_op jit(solution)/shard_map/all_to_all | solution.py:199
  371.1 8.9 %all_to_all.218 = f32[8,2,256]{2,1,0:T(2,128)S(1)} all-to-all(f32[8,2,256]{2,1,0:T(2,128)S(1)} %broadcast_in_dim.104), channel_id=1, replica_groups=mesh['x'=4,'core'=2,'z'=8,'y'=4] {'x','core'}, dimensions={0} | all-to-all | bytes 32768 | tf_op jit(solution)/shard_map/all_to_all | solution.py:199
  380.1 11.9 %all_to_all.219 = f32[32,2,256]{2,1,0:T(2,128)S(1)} all-to-all(f32[32,2,256]{2,1,0:T(2,128)S(1)} %broadcast_in_dim.105), channel_id=1, replica_groups=mesh['x'=4,'core'=2,'z'=8,'y'=4] {'z','y'}, dimensions={0} | all-to-all | bytes 131072 | tf_op jit(solution)/shard_map/all_to_all | solution.py:199
  392.4 8.9 %all_to_all.220 = f32[8,2,256]{2,1,0:T(2,128)S(1)} all-to-all(f32[8,2,256]{2,1,0:T(2,128)S(1)} %broadcast_in_dim.106), channel_id=1, replica_groups=mesh['x'=4,'core'=2,'z'=8,'y'=4] {'x','core'}, dimensions={0} | all-to-all | bytes 32768 | tf_op jit(solution)/shard_map/all_to_all | solution.py:199
  401.4 11.9 %all_to_all.221 = f32[32,2,256]{2,1,0:T(2,128)S(1)} all-to-all(f32[32,2,256]{2,1,0:T(2,128)S(1)} %broadcast_in_dim.107), channel_id=1, replica_groups=mesh['x'=4,'core'=2,'z'=8,'y'=4] {'z','y'}, dimensions={0} | all-to-all | bytes 131072 | tf_op jit(solution)/shard_map/all_to_all | solution.py:199
  413.7 9.1 %all_to_all.222 = f32[8,2,256]{2,1,0:T(2,128)S(1)} all-to-all(f32[8,2,256]{2,1,0:T(2,128)S(1)} %broadcast_in_dim.108), channel_id=1, replica_groups=mesh['x'=4,'core'=2,'z'=8,'y'=4] {'x','core'}, dimensions={0} | all-to-all | bytes 32768 | tf_op jit(solution)/shard_map/all_to_all | solution.py:199
  422.9 11.9 %all_to_all.223 = f32[32,2,256]{2,1,0:T(2,128)S(1)} all-to-all(f32[32,2,256]{2,1,0:T(2,128)S(1)} %broadcast_in_dim.109), channel_id=1, replica_groups=mesh['x'=4,'core'=2,'z'=8,'y'=4] {'z','y'}, dimensions={0} | all-to-all | bytes 131072 | tf_op jit(solution)/shard_map/all_to_all | solution.py:199
  435.2 8.9 %all_to_all.224 = f32[8,2,256]{2,1,0:T(2,128)S(1)} all-to-all(f32[8,2,256]{2,1,0:T(2,128)S(1)} %broadcast_in_dim.110), channel_id=1, replica_groups=mesh['x'=4,'core'=2,'z'=8,'y'=4] {'x','core'}, dimensions={0} | all-to-all | bytes 32768 | tf_op jit(solution)/shard_map/all_to_all | solution.py:199
  444.2 11.9 %all_to_all.225 = f32[32,2,256]{2,1,0:T(2,128)S(1)} all-to-all(f32[32,2,256]{2,1,0:T(2,128)S(1)} %broadcast_in_dim.111), channel_id=1, replica_groups=mesh['x'=4,'core'=2,'z'=8,'y'=4] {'z','y'}, dimensions={0} | all-to-all | bytes 131072 | tf_op jit(solution)/shard_map/all_to_all | solution.py:199
  456.5 8.9 %all_to_all.226 = f32[8,2,256]{2,1,0:T(2,128)S(1)} all-to-all(f32[8,2,256]{2,1,0:T(2,128)S(1)} %broadcast_in_dim.112), channel_id=1, replica_groups=mesh['x'=4,'core'=2,'z'=8,'y'=4] {'x','core'}, dimensions={0} | all-to-all | bytes 32768 | tf_op jit(solution)/shard_map/all_to_all | solution.py:199
  465.5 11.9 %all_to_all.227 = f32[32,2,256]{2,1,0:T(2,128)S(1)} all-to-all(f32[32,2,256]{2,1,0:T(2,128)S(1)} %broadcast_in_dim.113), channel_id=1, replica_groups=mesh['x'=4,'core'=2,'z'=8,'y'=4] {'z','y'}, dimensions={0} | all-to-all | bytes 131072 | tf_op jit(solution)/shard_map/all_to_all | solution.py:199
  478.0 1.4 shard_map.104
  (144 shorter events, 15.0 us)
Async XLA Ops:
  0.6 0.7 copy-start.14
  2.0 1.0 copy-start
  3.0 1.0 copy-start.2
  4.1 1.0 copy-start.12
  5.1 1.0 copy-start.13
  45.2 18.5 %copy-start.1 = (f32[512,256]{1,0:T(8,128)S(1)}, f32[512,256]{1,0:T(8,128)}, u32[]{:S(2)}) copy-start(f32[512,256]{1,0:T(8,128)} %x_ref.7) | copy-start | bytes 1572868
  45.2 18.5 %copy-start.3 = (f32[512,256]{1,0:T(8,128)S(1)}, f32[512,256]{1,0:T(8,128)}, u32[]{:S(2)}) copy-start(f32[512,256]{1,0:T(8,128)} %y_ref.7) | copy-start | bytes 1572868
  65.1 0.8 copy-start.8
  65.9 0.8 copy-start.10
  85.4 1.0 copy-start.9
  86.4 1.0 copy-start.11
  285.7 0.8 copy-start.4
  286.5 0.8 copy-start.6
  287.3 18.8 %copy-start.5 = (f32[256,512]{1,0:T(8,128)S(1)}, f32[256,512]{1,0:T(8,128)}, u32[]{:S(2)}) copy-start(f32[256,512]{1,0:T(8,128)} %copy-done.4) | copy-start | bytes 1572868
  306.1 1.0 copy-start.7
